TPU v7x, 32 devices: a whole 2x2x4 slice. The times are simulated.
32 devices in a mesh: prompt: 4 (over x, core), resp: 8 (over z, y).
Axes of the slice: x: 2, y: 2, z: 4, core: 2. Of those that a mesh axis runs over, the one named last changes fastest.
Arguments:
- queries: bfloat16 [32, 256, 4096], P(('prompt', 'resp')), may hold values from -5 to 5
- resp_keys: bfloat16 [32, 256, 512], P(('prompt', 'resp')), may hold values from -6 to 6
- resp_values: bfloat16 [32, 256, 512], P(('prompt', 'resp')), may hold values from -6 to 6
- grad_out: bfloat16 [32, 256, 4096], P(('prompt', 'resp')), may hold values from -24 to 24
- prompt_keys: bfloat16 [4, 256, 512], P('prompt', 'resp'), may hold values from -5 to 5
- prompt_values: bfloat16 [4, 256, 512], P('prompt', 'resp'), may hold values from -6 to 6
- group_sizes: int32 [4], replicated, may hold values from 1 to 16, 32 in all
- slot_response: int32 [32], replicated, may hold values from 0 to 31, each once
- lengths: int32 [32], P(('prompt', 'resp')), may hold values from 1 to 256, as said below
Outputs:
- grad_queries: bfloat16 [32, 256, 4096], P(('prompt', 'resp'))
- grad_resp_keys: bfloat16 [32, 256, 512], P(('prompt', 'resp'))
- grad_resp_values: bfloat16 [32, 256, 512], P(('prompt', 'resp'))
- grad_prompt_keys: float32 [4, 256, 512], P('prompt', 'resp')
- grad_prompt_values: float32 [4, 256, 512], P('prompt', 'resp')
Inputs may be any that keep to these rules, and one draw needn't show every extreme that they name: `group_sizes`: group sizes sum to 32; a group may hold a single response; the largest is exactly 16. `slot_response`: each response appears in exactly one slot. `lengths`: some response block is full.
All inputs are finite; a program needn't handle non-finite values.
Results may differ from a plain program's by a relative error of at most 0.012.
Values may be sent and summed in bfloat16 or wider, within the bound.
A program may use at most 128 MiB of HBM per device.

v0:
```python
import math

import jax
import jax.numpy as jnp
from jax import lax
from jax.sharding import PartitionSpec as P

KVH = 4
HD = 128
GRP = 8


def head_grads(query, key_rows, value_rows, upstream, allowed, scaling):
    scores = (
        jnp.einsum("tgh,jh->gtj", query, key_rows, preferred_element_type=jnp.float32) * scaling
    )
    scores = jnp.where(allowed[None], scores, -jnp.inf)
    row_max = jnp.max(scores, axis=-1, keepdims=True)
    unnorm = jnp.exp(scores - row_max)
    probs = unnorm / jnp.sum(unnorm, axis=-1, keepdims=True)
    probs_low = probs.astype(jnp.bfloat16)
    attended = jnp.einsum("gtj,jh->tgh", probs_low, value_rows, preferred_element_type=jnp.float32)
    row_dot = jnp.sum(upstream.astype(jnp.float32) * attended, axis=-1)
    dprob = jnp.einsum("tgh,jh->gtj", upstream, value_rows, preferred_element_type=jnp.float32)
    dscore = (probs * (dprob - jnp.transpose(row_dot)[:, :, None])).astype(jnp.bfloat16)
    grad_q = (
        jnp.einsum("gtj,jh->tgh", dscore, key_rows, preferred_element_type=jnp.float32) * scaling
    )
    grad_k = jnp.einsum("gtj,tgh->jh", dscore, query, preferred_element_type=jnp.float32) * scaling
    grad_v = jnp.einsum("gtj,tgh->jh", probs_low, upstream, preferred_element_type=jnp.float32)
    return (grad_q, grad_k, grad_v)


def attend(query, prompt_k, prompt_v, resp_k, resp_v, upstream, length):
    tok_count = query.shape[0]
    prompt_len = prompt_k.shape[0]
    scaling = 1.0 / math.sqrt(HD)
    key_rows = jnp.concatenate([prompt_k, resp_k], 0)
    value_rows = jnp.concatenate([prompt_v, resp_v], 0)
    row_ids = jnp.arange(tok_count)[:, None]
    col_ids = jnp.arange(prompt_len + tok_count)[None, :] - prompt_len
    allowed = (col_ids < 0) | (col_ids <= row_ids) & (col_ids < length)
    live_rows = jnp.arange(tok_count) < length
    upstream = jnp.where(live_rows[:, None], upstream, jnp.zeros_like(upstream))
    query_heads = query.reshape(tok_count, KVH, GRP, HD)
    upstream_heads = upstream.reshape(tok_count, KVH, GRP, HD)
    q_parts, k_parts, v_parts = ([], [], [])
    for kv_head in range(KVH):
        lower = kv_head * HD
        grad_q, grad_k, grad_v = head_grads(
            query_heads[:, kv_head],
            key_rows[:, lower : lower + HD],
            value_rows[:, lower : lower + HD],
            upstream_heads[:, kv_head],
            allowed,
            scaling,
        )
        q_parts.append(grad_q)
        k_parts.append(grad_k)
        v_parts.append(grad_v)
    grad_q = jnp.stack(q_parts, axis=1).reshape(tok_count, KVH * GRP * HD).astype(jnp.bfloat16)
    grad_k = jnp.concatenate(k_parts, axis=1)
    grad_v = jnp.concatenate(v_parts, axis=1)
    return (
        grad_q,
        grad_k[:prompt_len],
        grad_v[:prompt_len],
        grad_k[prompt_len:].astype(jnp.bfloat16),
        grad_v[prompt_len:].astype(jnp.bfloat16),
    )


def per_device(
    queries,
    resp_keys,
    resp_values,
    grad_out,
    prompt_keys,
    prompt_values,
    group_sizes,
    slot_response,
    lengths,
):
    rows_each = prompt_keys.shape[1]
    width = prompt_keys.shape[2]
    resp_count = lax.axis_size("resp")
    prompt_count = lax.axis_size("prompt")
    prompt_len = rows_each * resp_count
    group_ends = jnp.cumsum(group_sizes)
    prompt_of = jnp.sum((slot_response[:, None] >= group_ends[None, :]).astype(jnp.int32), axis=1)
    column = lax.axis_index("prompt")
    own_slot = column * resp_count + lax.axis_index("resp")
    own_prompt = prompt_of[own_slot]
    every_k, every_v = (
        lax.all_gather(
            prompt_keys.reshape(rows_each, width), ("prompt", "resp"), axis=0, tiled=True
        ),
        lax.all_gather(
            prompt_values.reshape(rows_each, width), ("prompt", "resp"), axis=0, tiled=True
        ),
    )
    own_keys = lax.dynamic_slice_in_dim(every_k, own_prompt * prompt_len, prompt_len, 0)
    own_values = lax.dynamic_slice_in_dim(every_v, own_prompt * prompt_len, prompt_len, 0)
    grad_q, key_grad, value_grad, resp_kg, resp_vg = attend(
        queries[0], own_keys, own_values, resp_keys[0], resp_values[0], grad_out[0], lengths[0]
    )
    blank = jnp.zeros((prompt_count * prompt_len, width), jnp.float32)
    term_k = lax.dynamic_update_slice_in_dim(blank, key_grad, own_prompt * prompt_len, 0)
    term_v = lax.dynamic_update_slice_in_dim(blank, value_grad, own_prompt * prompt_len, 0)
    summed_k, summed_v = (
        lax.psum_scatter(term_k, ("prompt", "resp"), scatter_dimension=0, tiled=True),
        lax.psum_scatter(term_v, ("prompt", "resp"), scatter_dimension=0, tiled=True),
    )
    owned_k = summed_k.reshape(1, rows_each, width)
    owned_v = summed_v.reshape(1, rows_each, width)
    return (grad_q[None], resp_kg[None], resp_vg[None], owned_k, owned_v)


def solution(mesh):
    in_specs = (
        P(("prompt", "resp"), None, None),
        P(("prompt", "resp"), None, None),
        P(("prompt", "resp"), None, None),
        P(("prompt", "resp"), None, None),
        P("prompt", "resp", None),
        P("prompt", "resp", None),
        P(),
        P(),
        P(("prompt", "resp")),
    )
    out_specs = (
        P(("prompt", "resp"), None, None),
        P(("prompt", "resp"), None, None),
        P(("prompt", "resp"), None, None),
        P("prompt", "resp", None),
        P("prompt", "resp", None),
    )
    return jax.shard_map(
        per_device, mesh=mesh, in_specs=in_specs, out_specs=out_specs, check_vma=False
    )
```

profile of v0, /device:TPU:0, one launch (start us, length us, event | category | flops | bytes accessed | tf_op | source)
XLA Modules:
  0.0 439.8 jit_solution(13530718154746471498)
XLA Ops:
  12.2 3.3 copy.103
  15.5 4.5 %copy.105 = bf16[1,256,4096]{1,2,0:T(8,128)(2,1)} copy(bf16[1,256,4096]{2,1,0:T(8,128)(2,1)} %param.12) | data formatting | bytes 4194304 | tf_op args[3]
  20.0 4.0 copy.106
  24.3 3.2 broadcast_select_fusion
  27.5 40.1 %all-gather.5.cloned.1.call-done = bf16[1,1024,512]{2,1,0:T(8,128)(2,1)} async-done(((bf16[1,32,512]{2,1,0:T(8,128)(2,1)}), bf16[1,1024,512]{2,1,0:T(8,128)(2,1)}) %all-gather.5.cloned.1.call-update) | async-done | bytes 1048592 | tf_op jit(solution)/shard_map/all_gather | solution.py:95
  68.6 2.7 fusion.56
  71.3 2.7 fusion.55
  74.0 2.6 fusion.54
  76.6 46.8 %all-gather.7.cloned.1.call-done = bf16[1,1024,512]{2,1,0:T(8,128)(2,1)} async-done(((bf16[1,32,512]{2,1,0:T(8,128)(2,1)}), bf16[1,1024,512]{2,1,0:T(8,128)(2,1)}) %all-gather.7.cloned.1.call-update) | async-done | bytes 1048592 | tf_op jit(solution)/shard_map/all_gather | solution.py:98
  124.4 5.2 %fusion.109 = (f32[8,256]{1,0:T(8,128)S(1)}, f32[8,256,512]{1,2,0:T(8,128)S(1)}) fusion(f32[512,256,8]{1,0,2:T(8,128)} %fusion.56, pred[256,512]{0,1:T(8,128)(4,1)S(1)} %fusion.53), kind=kOutput, calls=%fused_computation.165 | output fusion | flops 6291967 | bytes 8527872 | tf_op jit(solution)/shard_map/sub | solution.py:19
  133.1 1.4 copy-done.16
  135.9 1.8 fusion.110
  142.2 2.0 fusion.111
  148.4 1.8 fusion.108
  156.9 1.6 broadcast_in_dim.72.clone
  159.4 2.0 convolution_bitcast_fusion.5
  161.5 2.0 convolution_bitcast_fusion.6
  163.5 2.0 convolution_bitcast_fusion.7
  165.6 1.9 convolution_bitcast_fusion.4
  169.1 1.3 copy-done.10
  170.5 2.2 fusion.45
  176.6 2.9 copy.148
  183.3 112.9 %reduce-scatter.3.cloned.1.call-done = f32[32,512]{1,0:T(8,128)} async-done(((f32[1024,512]{1,0:T(8,128)}), f32[32,512]{1,0:T(8,128)}) %reduce-scatter.3.cloned.1.call-update) | async-done | bytes 65552 | tf_op jit(solution)/shard_map/reduce_scatter | solution.py:111
  296.3 137.0 %reduce-scatter.5.cloned.1.call-done = f32[32,512]{1,0:T(8,128)} async-done(((f32[1024,512]{1,0:T(8,128)}), f32[32,512]{1,0:T(8,128)}) %reduce-scatter.5.cloned.1.call-update) | async-done | bytes 65552 | tf_op jit(solution)/shard_map/reduce_scatter | solution.py:112
  (97 shorter events, 36.2 us)
Async XLA Ops:
  7.2 60.5 %all-gather.5.cloned.1.call-start = ((), (), s32[]{:S(2)}) async-start(), calls=%async_computation.4 | async-start | bytes 1081344 | tf_op jit(solution)/shard_map/all_gather | solution.py:95
  7.9 115.5 %all-gather.7.cloned.1.call-start = ((), (), s32[]{:S(2)}) async-start(), calls=%async_computation.5 | async-start | bytes 1081344 | tf_op jit(solution)/shard_map/all_gather | solution.py:98
  8.7 287.6 %reduce-scatter.3.cloned.1.call-start = ((), (), s32[]{:S(2)}) async-start(), calls=%async_computation.2 | async-start | bytes 2162688 | tf_op jit(solution)/shard_map/reduce_scatter | solution.py:111
  15.5 58.5 %copy-start.6 = (bf16[1,256,4096]{1,2,0:T(8,128)(2,1)}, bf16[1,256,4096]{1,2,0:T(8,128)(2,1)S(1)}, u32[]{:S(2)}) copy-start(bf16[1,256,4096]{1,2,0:T(8,128)(2,1)S(1)} %copy.103) | copy-start | bytes 6291460
  24.3 44.3 %copy-start.5 = (bf16[1,256,512]{2,1,0:T(8,128)(2,1)S(1)}, bf16[1,256,512]{2,1,0:T(8,128)(2,1)}, u32[]{:S(2)}) copy-start(bf16[1,256,512]{2,1,0:T(8,128)(2,1)} %param.10) | copy-start | bytes 786436
  74.0 50.4 %copy-start.11 = (bf16[1,256,512]{2,1,0:T(8,128)(2,1)S(1)}, bf16[1,256,512]{2,1,0:T(8,128)(2,1)}, u32[]{:S(2)}) copy-start(bf16[1,256,512]{2,1,0:T(8,128)(2,1)} %param.11) | copy-start | bytes 786436
  129.6 1.6 copy-start.4
  132.3 2.1 copy-start.7
  132.3 3.6 copy-start.13
  133.0 1.4 copy-start.16
  138.1 1.9 copy-start
  139.2 2.9 copy-start.12
  139.9 1.3 copy-start.17
  144.5 1.8 copy-start.2
  146.4 1.3 copy-start.19
  150.7 1.8 copy-start.8
  159.4 273.9 %reduce-scatter.5.cloned.1.call-start = ((), (), s32[]{:S(2)}) async-start(), calls=%async_computation.3 | async-start | bytes 2162688 | tf_op jit(solution)/shard_map/reduce_scatter | solution.py:112
  159.4 2.0 copy-start.1
  161.5 2.0 copy-start.3
  163.5 2.0 copy-start.9
  169.1 1.4 copy-start.10
  170.4 2.2 copy-start.18
  172.7 1.6 copy-start.20
  174.3 1.6 copy-start.22
  (3 other events, 3.3 us)
Sparse Core Ops, SparseCore 0:
  11.1 56.5 all-gather.4
  70.7 52.6 all-gather.6
  159.5 136.7 reduce-scatter.2
  299.1 134.1 reduce-scatter.4
where the time goes:
time: 441 us; the launch traced here: 440 us
  waiting for transfers between devices  338 us (77%)
  local copies, waits for them, and re-layouts  37.3 us (8%)
  matrix products  30.7 us (7%)
  other arithmetic  17.8 us (4%)
  between operations  15.6 us (4%)
    reduce_scatter x1, waiting for transfers between devices, per_device(): lax.psum_scatter(term_v, ('prompt', 'resp'), scatter_dimension=0, tiled=T...  137 us
    reduce_scatter x1, waiting for transfers between devices, per_device(): lax.psum_scatter(term_k, ('prompt', 'resp'), scatter_dimension=0, tiled=T...  113 us
    all_gather x1, waiting for transfers between devices, per_device(): lax.all_gather(prompt_values.reshape(rows_each, width), ('prompt', 'resp'...  46.8 us
    all_gather x1, waiting for transfers between devices, per_device(): lax.all_gather(prompt_keys.reshape(rows_each, width), ('prompt', 'resp'),...  40.1 us
    unnamed x51, local copies, waits for them, and re-layouts  23.6 us
    sub x4, other arithmetic, head_grads(): unnorm = jnp.exp(scores - row_max)  10.9 us
  transfers between devices with their start and end apart: 4, of which 4 were waited for; matrix products, arithmetic and copies ran while one was open for 10% of the time, Pallas kernels for 0%

commit v1 on v0

v1 whole, which is shorter than its diff:
```python
import functools
import math

import jax
import jax.numpy as jnp
from jax import lax
from jax.experimental import pallas as pl
from jax.experimental.pallas import tpu as pltpu
from jax.sharding import PartitionSpec as P

HD = 128
GRP = 8
MESH = pl.DeviceIdType.MESH
F32 = jnp.float32
BF16 = jnp.bfloat16


def nt(a, b):
    return lax.dot_general(a, b, (((1,), (1,)), ((), ())), preferred_element_type=F32)


def nn(a, b):
    return jnp.dot(a, b, preferred_element_type=F32)


def kernel(
    n_p,
    n_r,
    q_hbm,
    do_hbm,
    rk_ref,
    rv_ref,
    pk_ref,
    pv_ref,
    sizes_ref,
    slot_ref,
    len_ref,
    gq_hbm,
    grk_ref,
    grv_ref,
    gpk_ref,
    gpv_ref,
    q_v,
    do_v,
    gq_v,
    g1,
    s2,
    r2,
    sa,
    ra,
    sb,
    rb,
    kbuf,
    vbuf,
    ktbuf,
    gk_acc,
    gv_acc,
    in_sem,
    out_sem,
    g1_send,
    g1_recv,
    s2_send,
    s2_recv,
    a_send,
    a_recv,
    b_send,
    b_recv,
):
    c = lax.axis_index("prompt")
    r = lax.axis_index("resp")
    rows = pk_ref.shape[1]
    kv_heads = pk_ref.shape[2] // HD
    tok = rk_ref.shape[1]
    plen = rows * n_r
    half = tok // 2
    top = plen + half
    scaling = 1.0 / math.sqrt(HD)
    to_exp2 = scaling * math.log2(math.e)

    def column_peer(i):
        return lax.rem(c + i, n_p)

    def row_peer(i):
        return lax.rem(r + i, n_r)

    def prompt_of(resp_index):
        value = slot_ref[c * n_r + resp_index]
        end = sizes_ref[0]
        found = (value >= end).astype(jnp.int32)
        for k in range(1, n_p - 1):
            end = end + sizes_ref[k]
            found = found + (value >= end).astype(jnp.int32)
        return found

    q_in = pltpu.make_async_copy(q_hbm.at[0], q_v, in_sem.at[0])
    do_in = pltpu.make_async_copy(do_hbm.at[0], do_v, in_sem.at[1])
    q_in.start()
    do_in.start()

    barrier = pltpu.get_barrier_semaphore()
    for i in range(1, n_p):
        pl.semaphore_signal(barrier, inc=1, device_id=(column_peer(i), r), device_id_type=MESH)
    for i in range(1, n_r):
        pl.semaphore_signal(barrier, inc=1, device_id=(c, row_peer(i)), device_id_type=MESH)
    g1[c, 0] = pk_ref[0]
    g1[c, 1] = pv_ref[0]
    pl.semaphore_wait(barrier, n_p + n_r - 2)

    def gather_first(to, slot):
        return pltpu.make_async_remote_copy(
            src_ref=g1.at[slot],
            dst_ref=g1.at[slot],
            send_sem=g1_send.at[to],
            recv_sem=g1_recv.at[slot],
            device_id=(to, r),
            device_id_type=MESH,
        )

    def gather_second(kv, to, slot):
        return pltpu.make_async_remote_copy(
            src_ref=s2.at[kv, to],
            dst_ref=r2.at[kv, slot],
            send_sem=s2_send.at[kv, to],
            recv_sem=s2_recv.at[kv, slot],
            device_id=(c, to),
            device_id_type=MESH,
        )

    def sum_first(kv, to, slot):
        return pltpu.make_async_remote_copy(
            src_ref=sa.at[kv, to],
            dst_ref=ra.at[kv, slot],
            send_sem=a_send.at[kv, to],
            recv_sem=a_recv.at[kv, slot],
            device_id=(c, to),
            device_id_type=MESH,
        )

    def sum_second(kv, to, slot):
        return pltpu.make_async_remote_copy(
            src_ref=sb.at[kv, to],
            dst_ref=rb.at[kv, slot],
            send_sem=b_send.at[kv, to],
            recv_sem=b_recv.at[kv, slot],
            device_id=(to, r),
            device_id_type=MESH,
        )

    for i in range(1, n_p):
        gather_first(column_peer(i), c).start()
    for i in range(1, n_p):
        gather_first(column_peer(i), column_peer(i)).wait_recv()
    for kv in range(kv_heads):
        lanes = slice(kv * HD, (kv + 1) * HD)
        for i in range(1, n_r):
            to = row_peer(i)
            s2[kv, to] = g1[prompt_of(to), :, :, lanes]
            gather_second(kv, to, r).start()
        r2[kv, r] = g1[prompt_of(r), :, :, lanes]

    length = len_ref[0]
    live_mask = lax.broadcasted_iota(jnp.int32, (tok, HD), 0) < length
    causal = lax.broadcasted_iota(jnp.int32, (half, half), 0) <= lax.broadcasted_iota(
        jnp.int32, (half, half), 1
    )

    def one_head(head):
        lanes = pl.ds(pl.multiple_of(head * HD, HD), HD)
        q = q_v[:, lanes]
        live = jnp.where(live_mask, do_v[:, lanes], jnp.zeros((), BF16))
        q_b = q[half:]
        live_b = live[half:]
        s_a = nt(kbuf[:top], q)
        s_b = nt(kbuf[top:], q_b)
        s_p = s_a[:plen]
        s_c0 = jnp.where(causal, s_a[plen:, :half], -jnp.inf)
        s_c = jnp.concatenate([s_c0, s_a[plen:, half:]], axis=1)
        s_b = jnp.where(causal, s_b, -jnp.inf)
        m_a = jnp.maximum(
            jnp.max(s_p, axis=0, keepdims=True), jnp.max(s_c, axis=0, keepdims=True)
        )
        m_b = jnp.maximum(m_a[:, half:], jnp.max(s_b, axis=0, keepdims=True))
        m = jnp.concatenate([m_a[:, :half], m_b], axis=1) * to_exp2
        e_p = jnp.exp2(s_p * to_exp2 - m)
        e_c = jnp.exp2(s_c * to_exp2 - m)
        e_b = jnp.exp2(s_b * to_exp2 - m[:, half:])
        d_a = nt(vbuf[:top], live)
        d_b = nt(vbuf[top:], live_b)
        d_p = d_a[:plen]
        d_c = d_a[plen:]

        def total(a, b, low):
            first = jnp.sum(a, axis=0, keepdims=True) + jnp.sum(b, axis=0, keepdims=True)
            second = first[:, half:] + jnp.sum(low, axis=0, keepdims=True)
            return jnp.concatenate([first[:, :half], second], axis=1)

        inv = 1.0 / total(e_p, e_c, e_b)
        dot_row = total(e_p * d_p, e_c * d_c, e_b * d_b) * inv
        p_p = e_p * inv
        p_c = e_c * inv
        p_b = e_b * inv[:, half:]
        ds_p = (p_p * (d_p - dot_row)).astype(BF16)
        ds_c = (p_c * (d_c - dot_row)).astype(BF16)
        ds_b = (p_b * (d_b - dot_row[:, half:])).astype(BF16)
        gk_acc[:plen] += nn(ds_p, q)
        gk_acc[plen:top] += nn(ds_c, q)
        gk_acc[top:] += nn(ds_b, q_b)
        gv_acc[:plen] += nn(p_p.astype(BF16), live)
        gv_acc[plen:top] += nn(p_c.astype(BF16), live)
        gv_acc[top:] += nn(p_b.astype(BF16), live_b)
        g_a = nn(ktbuf[:, :plen], ds_p) + nn(ktbuf[:, plen:top], ds_c)
        g_b = g_a[:, half:] + nn(ktbuf[:, top:], ds_b)
        g_t = jnp.concatenate([g_a[:, :half], g_b], axis=1) * scaling
        gq_v[:, lanes] = jnp.transpose(g_t).astype(BF16)

    def attend(kv):
        lanes = slice(kv * HD, (kv + 1) * HD)
        for i in range(1, n_r):
            gather_second(kv, row_peer(i), row_peer(i)).wait_recv()
        kbuf[:plen] = r2[kv, :, 0].reshape(plen, HD)
        vbuf[:plen] = r2[kv, :, 1].reshape(plen, HD)
        kbuf[plen:] = rk_ref[0, :, lanes]
        vbuf[plen:] = rv_ref[0, :, lanes]
        ktbuf[...] = jnp.transpose(kbuf[...].astype(F32)).astype(BF16)
        gk_acc[...] = jnp.zeros_like(gk_acc)
        gv_acc[...] = jnp.zeros_like(gv_acc)

        def step(g, carry):
            one_head(kv * GRP + 2 * g)
            one_head(kv * GRP + 2 * g + 1)
            return carry

        lax.fori_loop(0, GRP // 2, step, 0)
        grad_k = gk_acc[...] * scaling
        grad_v = gv_acc[...]
        sa[kv, :, 0] = grad_k[:plen].astype(BF16).reshape(n_r, rows, HD)
        sa[kv, :, 1] = grad_v[:plen].astype(BF16).reshape(n_r, rows, HD)
        for i in range(1, n_r):
            sum_first(kv, row_peer(i), r).start()
        ra[kv, r] = sa[kv, r]
        grk_ref[0, :, lanes] = grad_k[plen:].astype(BF16)
        grv_ref[0, :, lanes] = grad_v[plen:].astype(BF16)
        gq_out(kv).start()

    def gq_out(kv):
        cols = pl.ds(kv * GRP * HD, GRP * HD)
        return pltpu.make_async_copy(gq_v.at[:, cols], gq_hbm.at[0, :, cols], out_sem.at[kv])

    def combine(kv):
        for i in range(1, n_r):
            sum_first(kv, row_peer(i), row_peer(i)).wait_recv()
        sums = [jnp.zeros((2, rows, HD), F32) for _ in range(n_p)]
        for src in range(n_r):
            owner = prompt_of(src)
            term = ra[kv, src].astype(F32)
            for p in range(n_p):
                sums[p] = sums[p] + jnp.where(owner == p, term, 0.0)
        for p in range(n_p):
            sb[kv, p] = sums[p]
        for i in range(1, n_p):
            sum_second(kv, column_peer(i), c).start()

    def finish(kv):
        lanes = slice(kv * HD, (kv + 1) * HD)
        out = sb[kv, c]
        for i in range(1, n_p):
            sum_second(kv, column_peer(i), column_peer(i)).wait_recv()
            out = out + rb[kv, column_peer(i)]
        gpk_ref[0, :, lanes] = out[0]
        gpv_ref[0, :, lanes] = out[1]

    q_in.wait()
    do_in.wait()
    for kv in range(kv_heads):
        attend(kv)
        if kv >= 1:
            combine(kv - 1)
        if kv >= 2:
            finish(kv - 2)
    combine(kv_heads - 1)
    for kv in range(max(kv_heads - 2, 0), kv_heads):
        finish(kv)

    for i in range(1, n_p):
        gather_first(column_peer(i), c).wait_send()
    for kv in range(kv_heads):
        gq_out(kv).wait()
        for i in range(1, n_r):
            gather_second(kv, row_peer(i), r).wait_send()
            sum_first(kv, row_peer(i), r).wait_send()
        for i in range(1, n_p):
            sum_second(kv, column_peer(i), c).wait_send()


def per_device(
    queries,
    resp_keys,
    resp_values,
    grad_out,
    prompt_keys,
    prompt_values,
    group_sizes,
    slot_response,
    lengths,
):
    n_p = lax.axis_size("prompt")
    n_r = lax.axis_size("resp")
    tok = queries.shape[1]
    width = queries.shape[2]
    rows = prompt_keys.shape[1]
    kv_width = prompt_keys.shape[2]
    kv_heads = kv_width // HD
    keys = rows * n_r + tok
    vmem = pl.BlockSpec(memory_space=pltpu.VMEM)
    smem = pl.BlockSpec(memory_space=pltpu.SMEM)
    anywhere = pl.BlockSpec(memory_space=pl.ANY)
    dma = pltpu.SemaphoreType.DMA
    return pl.pallas_call(
        functools.partial(kernel, n_p, n_r),
        out_shape=(
            jax.ShapeDtypeStruct(queries.shape, BF16),
            jax.ShapeDtypeStruct(resp_keys.shape, BF16),
            jax.ShapeDtypeStruct(resp_values.shape, BF16),
            jax.ShapeDtypeStruct(prompt_keys.shape, F32),
            jax.ShapeDtypeStruct(prompt_values.shape, F32),
        ),
        in_specs=[anywhere, anywhere, vmem, vmem, vmem, vmem, smem, smem, smem],
        out_specs=(anywhere, vmem, vmem, vmem, vmem),
        scratch_shapes=[
            pltpu.VMEM((tok, width), BF16),
            pltpu.VMEM((tok, width), BF16),
            pltpu.VMEM((tok, width), BF16),
            pltpu.VMEM((n_p, 2, rows, kv_width), BF16),
            pltpu.VMEM((kv_heads, n_r, 2, rows, HD), BF16),
            pltpu.VMEM((kv_heads, n_r, 2, rows, HD), BF16),
            pltpu.VMEM((kv_heads, n_r, 2, rows, HD), BF16),
            pltpu.VMEM((kv_heads, n_r, 2, rows, HD), BF16),
            pltpu.VMEM((kv_heads, n_p, 2, rows, HD), F32),
            pltpu.VMEM((kv_heads, n_p, 2, rows, HD), F32),
            pltpu.VMEM((keys, HD), BF16),
            pltpu.VMEM((keys, HD), BF16),
            pltpu.VMEM((HD, keys), BF16),
            pltpu.VMEM((keys, HD), F32),
            pltpu.VMEM((keys, HD), F32),
            dma((2,)),
            dma((kv_heads,)),
            dma((n_p,)),
            dma((n_p,)),
            dma((kv_heads, n_r)),
            dma((kv_heads, n_r)),
            dma((kv_heads, n_r)),
            dma((kv_heads, n_r)),
            dma((kv_heads, n_p)),
            dma((kv_heads, n_p)),
        ],
        compiler_params=pltpu.CompilerParams(
            collective_id=0, has_side_effects=True, vmem_limit_bytes=40 * 1024 * 1024
        ),
        cost_estimate=pl.CostEstimate(
            flops=10 * tok * keys * width,
            bytes_accessed=4 * tok * width * 2,
            transcendentals=tok * keys * width // HD,
        ),
    )(
        queries,
        grad_out,
        resp_keys,
        resp_values,
        prompt_keys,
        prompt_values,
        group_sizes,
        slot_response,
        lengths,
    )


def solution(mesh):
    in_specs = (
        P(("prompt", "resp"), None, None),
        P(("prompt", "resp"), None, None),
        P(("prompt", "resp"), None, None),
        P(("prompt", "resp"), None, None),
        P("prompt", "resp", None),
        P("prompt", "resp", None),
        P(),
        P(),
        P(("prompt", "resp")),
    )
    out_specs = (
        P(("prompt", "resp"), None, None),
        P(("prompt", "resp"), None, None),
        P(("prompt", "resp"), None, None),
        P("prompt", "resp", None),
        P("prompt", "resp", None),
    )
    return jax.shard_map(
        per_device, mesh=mesh, in_specs=in_specs, out_specs=out_specs, check_vma=False
    )
```

time: 441 us -> 62.7 us (0.14)
  waiting for transfers between devices: 338 us -> 0 us
  Pallas kernels: 0 us -> 49.1 us
  matrix products: 30.7 us -> 0 us
  local copies, waits for them, and re-layouts: 37.3 us -> 11.9 us
  other arithmetic: 17.8 us -> 0 us
  between operations: 15.6 us -> 1.31 us
    reduce_scatter x2 -> x0, waiting for transfers between devices: 250 us -> none  [the longest x1 137 us: per_device(): lax.psum_scatter(term_v, ('prompt', 'resp'), scatter_dimension=0, tiled=T...]
    all_gather x2 -> x0, waiting for transfers between devices: 87 us -> none  [the longest x1 46.8 us: per_device(): lax.all_gather(prompt_values.reshape(rows_each, width), ('prompt', 'resp'...]
    pallas_call x0 -> x1, Pallas kernels: none -> 49.1 us  [per_device(): pl.pallas_call(functools.partial(kernel, n_p, n_r), out_shape=(jax.ShapeD...]
    dot_general x24 -> x0, matrix products: 30.7 us -> none  [the longest x4 8.65 us: head_grads(): jnp.einsum('tgh,jh->gtj', query, key_rows, preferred_element_type=jnp.flo...]
    unnamed x51 -> x21, local copies, waits for them, and re-layouts: 23.6 us -> 11.9 us
    sub x5 -> x0, other arithmetic: 10.9 us -> none  [the longest x4 10.9 us: head_grads(): unnorm = jnp.exp(scores - row_max)]
  transfers between devices with their start and end apart: 4 -> 0, of which waited for: 4 -> 0; matrix products, arithmetic and copies ran while one was open for 10% -> 0% of each run, Pallas kernels for 0% -> 0%
where the time goes in v1:
time: 62.7 us; the launch traced here: 62.3 us
  Pallas kernels  49.1 us (78%)
  local copies, waits for them, and re-layouts  11.9 us (19%)
  between operations  1.31 us (2%)
    pallas_call x1, Pallas kernels, per_device(): pl.pallas_call(functools.partial(kernel, n_p, n_r), out_shape=(jax.ShapeD...  49.1 us
    unnamed x21, local copies, waits for them, and re-layouts  11.9 us

profile of v1, /device:TPU:0, one launch (start us, length us, event | category | flops | bytes accessed | tf_op | source)
XLA Modules:
  0.0 62.3 jit_solution(941203232809968682)
XLA Ops:
  1.3 0.0 copy-start
  1.3 1.6 %copy-done = bf16[1,256,4096]{2,1,0:T(8,128)(2,1)S(1)} copy-done((bf16[1,256,4096]{2,1,0:T(8,128)(2,1)S(1)}, bf16[1,256,4096]{2,1,0:T(8,128)(2,1)}, u32[]{:S(2)}) %copy-start) | copy-done | bytes 2097176
  2.9 0.0 copy-start.1
  2.9 1.6 %copy-done.1 = bf16[1,256,4096]{2,1,0:T(8,128)(2,1)S(1)} copy-done((bf16[1,256,4096]{2,1,0:T(8,128)(2,1)S(1)}, bf16[1,256,4096]{2,1,0:T(8,128)(2,1)}, u32[]{:S(2)}) %copy-start.1) | copy-done | bytes 2097176
  4.5 0.0 copy-start.2
  4.5 0.9 %copy-done.2 = bf16[1,256,512]{2,1,0:T(8,128)(2,1)S(1)} copy-done((bf16[1,256,512]{2,1,0:T(8,128)(2,1)S(1)}, bf16[1,256,512]{2,1,0:T(8,128)(2,1)}, u32[]{:S(2)}) %copy-start.2) | copy-done | bytes 262168
  5.4 0.0 copy-start.3
  5.4 0.9 %copy-done.3 = bf16[1,256,512]{2,1,0:T(8,128)(2,1)S(1)} copy-done((bf16[1,256,512]{2,1,0:T(8,128)(2,1)S(1)}, bf16[1,256,512]{2,1,0:T(8,128)(2,1)}, u32[]{:S(2)}) %copy-start.3) | copy-done | bytes 262168
  6.4 0.0 copy-start.4
  6.4 0.8 %copy-done.4 = bf16[1,32,512]{2,1,0:T(8,128)(2,1)S(1)} copy-done((bf16[1,32,512]{2,1,0:T(8,128)(2,1)S(1)}, bf16[1,32,512]{2,1,0:T(8,128)(2,1)}, u32[]{:S(2)}) %copy-start.4) | copy-done | bytes 32792
  7.1 0.0 copy-start.5
  7.1 0.8 %copy-done.5 = bf16[1,32,512]{2,1,0:T(8,128)(2,1)S(1)} copy-done((bf16[1,32,512]{2,1,0:T(8,128)(2,1)S(1)}, bf16[1,32,512]{2,1,0:T(8,128)(2,1)}, u32[]{:S(2)}) %copy-start.5) | copy-done | bytes 32792
  7.9 0.0 copy-start.6
  7.9 0.7 %copy-done.6 = s32[4]{0:T(128)S(1)} copy-done((s32[4]{0:T(128)S(1)}, s32[4]{0:T(128)}, u32[]{:S(2)}) %copy-start.6) | copy-done | bytes 40
  8.5 0.0 copy-start.7
  8.5 0.7 %copy-done.7 = s32[32]{0:T(128)S(1)} copy-done((s32[32]{0:T(128)S(1)}, s32[32]{0:T(128)}, u32[]{:S(2)}) %copy-start.7) | copy-done | bytes 152
  9.2 49.1 %shard_map.128 = (bf16[1,256,4096]{2,1,0:T(8,128)(2,1)S(1)}, bf16[1,256,512]{2,1,0:T(8,128)(2,1)S(1)}, bf16[1,256,512]{2,1,0:T(8,128)(2,1)S(1)}, f32[1,32,512]{2,1,0:T(8,128)S(1)}, f32[1,32,512]{2,1,0:T(8,128)S(1)}) custom-call(bf16[1,256,4096]{2,1,0:T(8,128)(2,1)S(1)} %copy-done, bf16[1,256,4096]{2,1,0:T(8,128)(2,1)S(1)} %copy-done.1, ...), custom_call_target="tpu_custom_call" | custom-call | flops 5368709120 | bytes 8388608 | tf_op jit(solution)/shard_map/pallas_call | solution.py:318
  58.3 1.3 %copy.20 = bf16[1,256,4096]{2,1,0:T(8,128)(2,1)} copy(bf16[1,256,4096]{2,1,0:T(8,128)(2,1)S(1)} %get-tuple-element.10) | data formatting | bytes 4194304
  59.7 0.7 %copy.21 = bf16[1,256,512]{2,1,0:T(8,128)(2,1)} copy(bf16[1,256,512]{2,1,0:T(8,128)(2,1)S(1)} %get-tuple-element.11) | data formatting | bytes 524288
  60.4 0.7 %copy.22 = bf16[1,256,512]{2,1,0:T(8,128)(2,1)} copy(bf16[1,256,512]{2,1,0:T(8,128)(2,1)S(1)} %get-tuple-element.12) | data formatting | bytes 524288
  61.1 0.6 %copy.23 = f32[1,32,512]{2,1,0:T(8,128)} copy(f32[1,32,512]{2,1,0:T(8,128)S(1)} %get-tuple-element.13) | data formatting | bytes 131072
  61.7 0.6 %copy.24 = f32[1,32,512]{2,1,0:T(8,128)} copy(f32[1,32,512]{2,1,0:T(8,128)S(1)} %get-tuple-element.14) | data formatting | bytes 131072
Async XLA Ops:
  1.3 1.6 %copy-start = (bf16[1,256,4096]{2,1,0:T(8,128)(2,1)S(1)}, bf16[1,256,4096]{2,1,0:T(8,128)(2,1)}, u32[]{:S(2)}) copy-start(bf16[1,256,4096]{2,1,0:T(8,128)(2,1)} %q_hbm.1) | copy-start | bytes 6291460
  2.9 1.6 %copy-start.1 = (bf16[1,256,4096]{2,1,0:T(8,128)(2,1)S(1)}, bf16[1,256,4096]{2,1,0:T(8,128)(2,1)}, u32[]{:S(2)}) copy-start(bf16[1,256,4096]{2,1,0:T(8,128)(2,1)} %do_hbm.1) | copy-start | bytes 6291460
  4.5 0.9 %copy-start.2 = (bf16[1,256,512]{2,1,0:T(8,128)(2,1)S(1)}, bf16[1,256,512]{2,1,0:T(8,128)(2,1)}, u32[]{:S(2)}) copy-start(bf16[1,256,512]{2,1,0:T(8,128)(2,1)} %rk_ref.1) | copy-start | bytes 786436
  5.4 0.9 %copy-start.3 = (bf16[1,256,512]{2,1,0:T(8,128)(2,1)S(1)}, bf16[1,256,512]{2,1,0:T(8,128)(2,1)}, u32[]{:S(2)}) copy-start(bf16[1,256,512]{2,1,0:T(8,128)(2,1)} %rv_ref.1) | copy-start | bytes 786436
  6.4 0.8 %copy-start.4 = (bf16[1,32,512]{2,1,0:T(8,128)(2,1)S(1)}, bf16[1,32,512]{2,1,0:T(8,128)(2,1)}, u32[]{:S(2)}) copy-start(bf16[1,32,512]{2,1,0:T(8,128)(2,1)} %pk_ref.1) | copy-start | bytes 98308
  7.1 0.8 %copy-start.5 = (bf16[1,32,512]{2,1,0:T(8,128)(2,1)S(1)}, bf16[1,32,512]{2,1,0:T(8,128)(2,1)}, u32[]{:S(2)}) copy-start(bf16[1,32,512]{2,1,0:T(8,128)(2,1)} %pv_ref.1) | copy-start | bytes 98308
  7.9 0.7 %copy-start.6 = (s32[4]{0:T(128)S(1)}, s32[4]{0:T(128)}, u32[]{:S(2)}) copy-start(s32[4]{0:T(128)} %sizes_ref.1) | copy-start | bytes 52
  8.5 0.7 %copy-start.7 = (s32[32]{0:T(128)S(1)}, s32[32]{0:T(128)}, u32[]{:S(2)}) copy-start(s32[32]{0:T(128)} %slot_ref.1) | copy-start | bytes 388

commit v2 on v1

v2 whole, which is shorter than its diff:
```python
import functools
import math

import jax
import jax.numpy as jnp
from jax import lax
from jax.experimental import pallas as pl
from jax.experimental.pallas import tpu as pltpu
from jax.sharding import PartitionSpec as P

HD = 128
GRP = 8
VMEM_LIMIT = 60 * 1024 * 1024
MESH = pl.DeviceIdType.MESH
F32 = jnp.float32
BF16 = jnp.bfloat16


def nt(a, b):
    return lax.dot_general(a, b, (((1,), (1,)), ((), ())), preferred_element_type=F32)


def nn(a, b):
    return jnp.dot(a, b, preferred_element_type=F32)


def kernel(
    n_p,
    n_r,
    q_hbm,
    do_hbm,
    rk_hbm,
    rv_hbm,
    pk_hbm,
    pv_hbm,
    sizes_hbm,
    slot_hbm,
    len_hbm,
    gq_out,
    grk_ref,
    grv_ref,
    gpk_ref,
    gpv_ref,
    q_v,
    do_v,
    gq_v,
    sizes_ref,
    slot_ref,
    len_ref,
    g1,
    s2,
    r2,
    sa,
    ra,
    sb,
    rb,
    kall,
    vall,
    ktall,
    gk_acc,
    gv_acc,
    s_0,
    s_1,
    d_0,
    d_1,
    p_0,
    p_1,
    ds_0,
    ds_1,
    m_0,
    m_1,
    in_sem,
    kv_sem,
    out_sem,
    g1_send,
    g1_recv,
    s2_send,
    s2_recv,
    a_send,
    a_recv,
    b_send,
    b_recv,
):
    c = lax.axis_index("prompt")
    r = lax.axis_index("resp")
    rows = g1.shape[2]
    kv_heads = kall.shape[0]
    heads = kv_heads * GRP
    tok = q_v.shape[0]
    plen = rows * n_r
    half = tok // 2
    top = plen + half
    keys = plen + tok
    scaling = 1.0 / math.sqrt(HD)
    to_exp2 = scaling * math.log2(math.e)

    def column_peer(i):
        return lax.rem(c + i, n_p)

    def row_peer(i):
        return lax.rem(r + i, n_r)

    def prompt_of(resp_index):
        value = slot_ref[c * n_r + resp_index]
        end = sizes_ref[0]
        found = (value >= end).astype(jnp.int32)
        for k in range(1, n_p - 1):
            end = end + sizes_ref[k]
            found = found + (value >= end).astype(jnp.int32)
        return found

    first = [
        pltpu.make_async_copy(pk_hbm.at[0], g1.at[c, 0], in_sem.at[0]),
        pltpu.make_async_copy(pv_hbm.at[0], g1.at[c, 1], in_sem.at[1]),
        pltpu.make_async_copy(sizes_hbm, sizes_ref, in_sem.at[2]),
        pltpu.make_async_copy(slot_hbm, slot_ref, in_sem.at[3]),
        pltpu.make_async_copy(len_hbm, len_ref, in_sem.at[4]),
    ]
    q_in = pltpu.make_async_copy(q_hbm.at[0], q_v, in_sem.at[5])
    do_in = pltpu.make_async_copy(do_hbm.at[0], do_v, in_sem.at[6])
    resp_in = []
    for kv in range(kv_heads):
        lanes = pl.ds(kv * HD, HD)
        resp_in.append(
            pltpu.make_async_copy(
                rk_hbm.at[0, :, lanes], kall.at[kv, pl.ds(plen, tok)], kv_sem.at[0, kv]
            )
        )
        resp_in.append(
            pltpu.make_async_copy(
                rv_hbm.at[0, :, lanes], vall.at[kv, pl.ds(plen, tok)], kv_sem.at[1, kv]
            )
        )
    for copy in first + [do_in, q_in] + resp_in:
        copy.start()

    barrier = pltpu.get_barrier_semaphore()
    for i in range(1, n_p):
        pl.semaphore_signal(barrier, inc=1, device_id=(column_peer(i), r), device_id_type=MESH)
    for i in range(1, n_r):
        pl.semaphore_signal(barrier, inc=1, device_id=(c, row_peer(i)), device_id_type=MESH)
    for copy in first:
        copy.wait()
    pl.semaphore_wait(barrier, n_p + n_r - 2)

    def gather_first(to, slot):
        return pltpu.make_async_remote_copy(
            src_ref=g1.at[slot],
            dst_ref=g1.at[slot],
            send_sem=g1_send.at[to],
            recv_sem=g1_recv.at[slot],
            device_id=(to, r),
            device_id_type=MESH,
        )

    def gather_second(kv, to, slot):
        return pltpu.make_async_remote_copy(
            src_ref=s2.at[kv, to],
            dst_ref=r2.at[kv, slot],
            send_sem=s2_send.at[kv, to],
            recv_sem=s2_recv.at[kv, slot],
            device_id=(c, to),
            device_id_type=MESH,
        )

    def sum_first(kv, to, slot):
        return pltpu.make_async_remote_copy(
            src_ref=sa.at[kv, to],
            dst_ref=ra.at[kv, slot],
            send_sem=a_send.at[kv, to],
            recv_sem=a_recv.at[kv, slot],
            device_id=(c, to),
            device_id_type=MESH,
        )

    def sum_second(kv, to, slot):
        return pltpu.make_async_remote_copy(
            src_ref=sb.at[kv, to],
            dst_ref=rb.at[kv, slot],
            send_sem=b_send.at[kv, to],
            recv_sem=b_recv.at[kv, slot],
            device_id=(to, r),
            device_id_type=MESH,
        )

    for i in range(1, n_p):
        gather_first(column_peer(i), c).start()
    gk_acc[...] = jnp.zeros_like(gk_acc)
    gv_acc[...] = jnp.zeros_like(gv_acc)
    for ref in (p_0, p_1, ds_0, ds_1):
        ref[...] = jnp.zeros_like(ref)
    for i in range(1, n_p):
        gather_first(column_peer(i), column_peer(i)).wait_recv()
    for kv in range(kv_heads):
        lanes = slice(kv * HD, (kv + 1) * HD)
        for i in range(1, n_r):
            to = row_peer(i)
            s2[kv, to] = g1[prompt_of(to), :, :, lanes]
            gather_second(kv, to, r).start()
        r2[kv, r] = g1[prompt_of(r), :, :, lanes]

    do_in.wait()
    live_mask = lax.broadcasted_iota(jnp.int32, (tok, HD), 0) < len_ref[0]

    def mask_rows(head, carry):
        lanes = pl.ds(pl.multiple_of(head * HD, HD), HD)
        do_v[:, lanes] = jnp.where(live_mask, do_v[:, lanes], jnp.zeros((), BF16))
        return carry

    lax.fori_loop(0, heads, mask_rows, 0)
    q_in.wait()
    for copy in resp_in:
        copy.wait()

    slots = ((s_0, d_0, p_0, ds_0, m_0), (s_1, d_1, p_1, ds_1, m_1))

    def head_lanes(head):
        return pl.ds(pl.multiple_of(head * HD, HD), HD)

    def load_keys(kv):
        for i in range(1, n_r):
            gather_second(kv, row_peer(i), row_peer(i)).wait_recv()
        kall[kv, :plen] = r2[kv, :, 0].reshape(plen, HD)
        vall[kv, :plen] = r2[kv, :, 1].reshape(plen, HD)
        ktall[kv] = jnp.transpose(kall[kv].astype(F32)).astype(BF16)

    def scores(head, slot):
        s_ref, m_ref = slot[0], slot[4]
        s = nt(kall[head // GRP], q_v[:, head_lanes(head)])
        causal = lax.broadcasted_iota(jnp.int32, (half, half), 0) <= lax.broadcasted_iota(
            jnp.int32, (half, half), 1
        )
        s_p = s[:plen]
        s_l = jnp.where(causal, s[plen:top, :half], -jnp.inf)
        s_r = s[plen:top, half:]
        s_b = jnp.where(causal, s[top:, half:], -jnp.inf)
        s_ref[:plen] = s_p
        s_ref[plen:top, :half] = s_l
        s_ref[plen:top, half:] = s_r
        s_ref[top:, half:] = s_b
        m_p = jnp.max(s_p, axis=0, keepdims=True)
        m_l = jnp.max(s_l, axis=0, keepdims=True)
        m_r = jnp.max(jnp.maximum(s_r, s_b), axis=0, keepdims=True)
        m_ref[...] = jnp.maximum(m_p, jnp.concatenate([m_l, m_r], axis=1)) * to_exp2

    def value_products(head, slot):
        slot[1][...] = nt(vall[head // GRP], do_v[:, head_lanes(head)])

    def add_key_grad(head, slot):
        gk_acc[head // GRP] += nn(slot[3][...], q_v[:, head_lanes(head)])

    def add_value_grad(head, slot):
        gv_acc[head // GRP] += nn(slot[2][...], do_v[:, head_lanes(head)])

    def query_grad(head, slot):
        g_t = nn(ktall[head // GRP], slot[3][...]) * scaling
        gq_v[:, head_lanes(head)] = jnp.transpose(g_t).astype(BF16)

    quarter = half // 2

    def blocks(side):
        limit = top if side == 0 else keys
        return [(low, low + quarter) for low in range(0, limit, quarter)]

    def column(side):
        return slice(side * half, (side + 1) * half)

    def fold(x):
        return jnp.sum(x.reshape(-1, 8, half), axis=0)

    def exponentials(slot, side):
        s_ref, d_ref, m_ref = slot[0], slot[1], slot[4]
        cols = column(side)
        m = m_ref[:, cols]
        norm = jnp.zeros((8, half), F32)
        dots = jnp.zeros((8, half), F32)
        for low, high in blocks(side):
            e = jnp.exp2(s_ref[low:high, cols] * to_exp2 - m)
            s_ref[low:high, cols] = e
            norm = norm + fold(e)
            dots = dots + fold(e * d_ref[low:high, cols])
        inv = 1.0 / jnp.sum(norm, axis=0, keepdims=True)
        return inv, jnp.sum(dots, axis=0, keepdims=True) * inv

    def differences(slot, side, inv, dot_row):
        s_ref, d_ref, p_ref, ds_ref = slot[:4]
        cols = column(side)
        for low, high in blocks(side):
            p = s_ref[low:high, cols] * inv
            p_ref[low:high, cols] = p.astype(BF16)
            ds_ref[low:high, cols] = (p * (d_ref[low:high, cols] - dot_row)).astype(BF16)

    def step(head, cur, other):
        ahead = jnp.minimum(head + 1, heads - 1)
        behind = jnp.maximum(head - 1, 0)
        scores(ahead, other)
        stats_0 = exponentials(cur, 0)
        add_key_grad(behind, other)
        stats_1 = exponentials(cur, 1)
        add_value_grad(behind, other)
        differences(cur, 0, *stats_0)
        query_grad(behind, other)
        differences(cur, 1, *stats_1)
        value_products(ahead, other)

    def send_sums(kv):
        grad_k = gk_acc[kv] * scaling
        grad_v = gv_acc[kv]
        sa[kv, :, 0] = grad_k[:plen].astype(BF16).reshape(n_r, rows, HD)
        sa[kv, :, 1] = grad_v[:plen].astype(BF16).reshape(n_r, rows, HD)
        for i in range(1, n_r):
            sum_first(kv, row_peer(i), r).start()
        ra[kv, r] = sa[kv, r]
        lanes = head_lanes(kv)
        grk_ref[0, :, lanes] = grad_k[plen:].astype(BF16)
        grv_ref[0, :, lanes] = grad_v[plen:].astype(BF16)
        store_queries(kv).start()

    def store_queries(kv):
        cols = pl.ds(pl.multiple_of(kv * GRP * HD, HD), GRP * HD)
        return pltpu.make_async_copy(gq_v.at[:, cols], gq_out.at[0, :, cols], out_sem.at[kv])

    def combine(kv):
        for i in range(1, n_r):
            sum_first(kv, row_peer(i), row_peer(i)).wait_recv()
        sums = [jnp.zeros((2, rows, HD), F32) for _ in range(n_p)]
        for src in range(n_r):
            owner = prompt_of(src)
            term = ra[kv, src].astype(F32)
            for p in range(n_p):
                sums[p] = sums[p] + jnp.where(owner == p, term, 0.0)
        for p in range(n_p):
            sb[kv, p] = sums[p]
        for i in range(1, n_p):
            sum_second(kv, column_peer(i), c).start()

    def finish(kv):
        lanes = head_lanes(kv)
        out = sb[kv, c]
        for i in range(1, n_p):
            sum_second(kv, column_peer(i), column_peer(i)).wait_recv()
            out = out + rb[kv, column_peer(i)]
        gpk_ref[0, :, lanes] = out[0]
        gpv_ref[0, :, lanes] = out[1]

    load_keys(0)
    scores(0, slots[0])
    value_products(0, slots[0])
    pairs = GRP // 2

    def pair(index, carry):
        kv = index // pairs
        place = index % pairs

        @pl.when((place == pairs - 1) & (kv < kv_heads - 1))
        def _():
            load_keys(kv + 1)

        @pl.when((place == 1) & (kv > 0))
        def _():
            send_sums(kv - 1)

        @pl.when((place == pairs - 1) & (kv > 0))
        def _():
            combine(kv - 1)

        step(2 * index, slots[0], slots[1])
        step(2 * index + 1, slots[1], slots[0])
        return carry

    lax.fori_loop(0, heads // 2, pair, 0)
    add_key_grad(heads - 1, slots[1])
    add_value_grad(heads - 1, slots[1])
    query_grad(heads - 1, slots[1])
    send_sums(kv_heads - 1)
    for kv in range(kv_heads - 1):
        finish(kv)
    combine(kv_heads - 1)
    finish(kv_heads - 1)

    for i in range(1, n_p):
        gather_first(column_peer(i), c).wait_send()
    for kv in range(kv_heads):
        store_queries(kv).wait()
        for i in range(1, n_r):
            gather_second(kv, row_peer(i), r).wait_send()
            sum_first(kv, row_peer(i), r).wait_send()
        for i in range(1, n_p):
            sum_second(kv, column_peer(i), c).wait_send()


def store_kernel(*refs):
    count = (len(refs) - 1) // 2
    sem = refs[-1]
    copies = [
        pltpu.make_async_copy(refs[k], refs[count + k], sem.at[k]) for k in range(count)
    ]
    for copy in copies:
        copy.start()
    for copy in copies:
        copy.wait()


def per_device(
    queries,
    resp_keys,
    resp_values,
    grad_out,
    prompt_keys,
    prompt_values,
    group_sizes,
    slot_response,
    lengths,
):
    n_p = lax.axis_size("prompt")
    n_r = lax.axis_size("resp")
    tok = queries.shape[1]
    width = queries.shape[2]
    rows = prompt_keys.shape[1]
    kv_width = prompt_keys.shape[2]
    kv_heads = kv_width // HD
    keys = rows * n_r + tok
    vmem = pl.BlockSpec(memory_space=pltpu.VMEM)
    hbm = pl.BlockSpec(memory_space=pltpu.HBM)
    anywhere = pl.BlockSpec(memory_space=pl.ANY)
    dma = pltpu.SemaphoreType.DMA
    out_shape = (
        jax.ShapeDtypeStruct(queries.shape, BF16),
        jax.ShapeDtypeStruct(resp_keys.shape, BF16),
        jax.ShapeDtypeStruct(resp_values.shape, BF16),
        jax.ShapeDtypeStruct(prompt_keys.shape, F32),
        jax.ShapeDtypeStruct(prompt_values.shape, F32),
    )
    results = pl.pallas_call(
        functools.partial(kernel, n_p, n_r),
        out_shape=out_shape,
        in_specs=[hbm] * 9,
        out_specs=(anywhere, vmem, vmem, vmem, vmem),
        scratch_shapes=[
            pltpu.VMEM((tok, width), BF16),
            pltpu.VMEM((tok, width), BF16),
            pltpu.VMEM((tok, width), BF16),
            pltpu.SMEM(group_sizes.shape, jnp.int32),
            pltpu.SMEM(slot_response.shape, jnp.int32),
            pltpu.SMEM(lengths.shape, jnp.int32),
            pltpu.VMEM((n_p, 2, rows, kv_width), BF16),
            pltpu.VMEM((kv_heads, n_r, 2, rows, HD), BF16),
            pltpu.VMEM((kv_heads, n_r, 2, rows, HD), BF16),
            pltpu.VMEM((kv_heads, n_r, 2, rows, HD), BF16),
            pltpu.VMEM((kv_heads, n_r, 2, rows, HD), BF16),
            pltpu.VMEM((kv_heads, n_p, 2, rows, HD), F32),
            pltpu.VMEM((kv_heads, n_p, 2, rows, HD), F32),
            pltpu.VMEM((kv_heads, keys, HD), BF16),
            pltpu.VMEM((kv_heads, keys, HD), BF16),
            pltpu.VMEM((kv_heads, HD, keys), BF16),
            pltpu.VMEM((kv_heads, keys, HD), F32),
            pltpu.VMEM((kv_heads, keys, HD), F32),
            pltpu.VMEM((keys, tok), F32),
            pltpu.VMEM((keys, tok), F32),
            pltpu.VMEM((keys, tok), F32),
            pltpu.VMEM((keys, tok), F32),
            pltpu.VMEM((keys, tok), BF16),
            pltpu.VMEM((keys, tok), BF16),
            pltpu.VMEM((keys, tok), BF16),
            pltpu.VMEM((keys, tok), BF16),
            pltpu.VMEM((1, tok), F32),
            pltpu.VMEM((1, tok), F32),
            dma((7,)),
            dma((2, kv_heads)),
            dma((kv_heads,)),
            dma((n_p,)),
            dma((n_p,)),
            dma((kv_heads, n_r)),
            dma((kv_heads, n_r)),
            dma((kv_heads, n_r)),
            dma((kv_heads, n_r)),
            dma((kv_heads, n_p)),
            dma((kv_heads, n_p)),
        ],
        compiler_params=pltpu.CompilerParams(
            collective_id=0, has_side_effects=True, vmem_limit_bytes=VMEM_LIMIT
        ),
        cost_estimate=pl.CostEstimate(
            flops=10 * tok * keys * width,
            bytes_accessed=4 * tok * width * 2,
            transcendentals=tok * keys * width // HD,
        ),
    )(
        queries,
        grad_out,
        resp_keys,
        resp_values,
        prompt_keys,
        prompt_values,
        group_sizes,
        slot_response,
        lengths,
    )
    return pl.pallas_call(
        store_kernel,
        out_shape=out_shape,
        in_specs=[anywhere] * len(out_shape),
        out_specs=(hbm,) * len(out_shape),
        scratch_shapes=[dma((len(out_shape),))],
        compiler_params=pltpu.CompilerParams(vmem_limit_bytes=VMEM_LIMIT),
    )(*results)


def solution(mesh):
    in_specs = (
        P(("prompt", "resp"), None, None),
        P(("prompt", "resp"), None, None),
        P(("prompt", "resp"), None, None),
        P(("prompt", "resp"), None, None),
        P("prompt", "resp", None),
        P("prompt", "resp", None),
        P(),
        P(),
        P(("prompt", "resp")),
    )
    out_specs = (
        P(("prompt", "resp"), None, None),
        P(("prompt", "resp"), None, None),
        P(("prompt", "resp"), None, None),
        P("prompt", "resp", None),
        P("prompt", "resp", None),
    )
    return jax.shard_map(
        per_device, mesh=mesh, in_specs=in_specs, out_specs=out_specs, check_vma=False
    )
```

time: 62.7 us -> 137 us (2.19)
  Pallas kernels: 49.1 us -> 136 us
  local copies, waits for them, and re-layouts: 11.9 us -> 0 us
    pallas_call x1 -> x2, Pallas kernels: 49.1 us -> 136 us  [the longest x1 84.5 us: per_device(): pl.pallas_call(store_kernel, out_shape=out_shape, in_specs=[anywhere] * l...]
    unnamed x21 -> x0, local copies, waits for them, and re-layouts: 11.9 us -> none
where the time goes in v2:
time: 137 us
  Pallas kernels  136 us (99%)
    pallas_call x1, Pallas kernels, per_device(): pl.pallas_call(store_kernel, out_shape=out_shape, in_specs=[anywhere] * l...  84.5 us
    pallas_call x1, Pallas kernels, per_device(): pl.pallas_call(functools.partial(kernel, n_p, n_r), out_shape=out_shape,...  51.5 us

profile of v2, /device:TPU:0, one launch (start us, length us, event | category | flops | bytes accessed | tf_op | source)
XLA Modules:
  0.0 137.3 jit_solution(16594691827221354571)
XLA Ops:
  1.3 51.5 %shard_map.128 = (bf16[1,256,4096]{2,1,0:T(8,128)(2,1)}, bf16[1,256,512]{2,1,0:T(8,128)(2,1)}, bf16[1,256,512]{2,1,0:T(8,128)(2,1)}, f32[1,32,512]{2,1,0:T(8,128)}, f32[1,32,512]{2,1,0:T(8,128)}) custom-call(bf16[1,256,4096]{2,1,0:T(8,128)(2,1)} %q_hbm.1, bf16[1,256,4096]{2,1,0:T(8,128)(2,1)} %do_hbm.1, bf16[1,256,512]{2,1,0:T(8,128)(2,1)} %rk_hbm.1, ...), custom_call_target="tpu_custom_call" | custom-call | flops 5368709120 | bytes 8388608 | tf_op jit(solution)/shard_map/pallas_call | solution.py:434
  52.8 84.5 %shard_map.129 = (bf16[1,256,4096]{2,1,0:T(8,128)(2,1)}, bf16[1,256,512]{2,1,0:T(8,128)(2,1)}, bf16[1,256,512]{2,1,0:T(8,128)(2,1)}, f32[1,32,512]{2,1,0:T(8,128)}, f32[1,32,512]{2,1,0:T(8,128)}) custom-call(bf16[1,256,4096]{2,1,0:T(8,128)(2,1)} %get-tuple-element.10.refs_0_, bf16[1,256,512]{2,1,0:T(8,128)(2,1)} %get-tuple-element.11.refs_1_, ...), custom_call_target="tpu_custom_call" | custom-call | tf_op jit(solution)/shard_map/pallas_call | solution.py:499

commit v3 on v2

v3 whole, which is shorter than its diff:
```python
import functools
import math

import jax
import jax.numpy as jnp
from jax import lax
from jax.experimental import pallas as pl
from jax.experimental.pallas import tpu as pltpu
from jax.sharding import PartitionSpec as P

HD = 128
GRP = 8
VMEM_LIMIT = 60 * 1024 * 1024
MESH = pl.DeviceIdType.MESH
F32 = jnp.float32
BF16 = jnp.bfloat16


def nt(a, b):
    return lax.dot_general(a, b, (((1,), (1,)), ((), ())), preferred_element_type=F32)


def nn(a, b):
    return jnp.dot(a, b, preferred_element_type=F32)


def places(n_p, n_r):
    c = lax.axis_index("prompt")
    r = lax.axis_index("resp")
    columns = [lax.rem(c + i, n_p) for i in range(1, n_p)]
    partners = [lax.rem(r + i, n_r) for i in range(1, n_r)]
    return c, r, columns, partners


def prompt_of(sizes_ref, slot_ref, n_p, index):
    value = slot_ref[index]
    end = sizes_ref[0]
    found = (value >= end).astype(jnp.int32)
    for k in range(1, n_p - 1):
        end = end + sizes_ref[k]
        found = found + (value >= end).astype(jnp.int32)
    return found


def greet(c, r, columns, partners):
    barrier = pltpu.get_barrier_semaphore()
    for to in columns:
        pl.semaphore_signal(barrier, inc=1, device_id=(to, r), device_id_type=MESH)
    for to in partners:
        pl.semaphore_signal(barrier, inc=1, device_id=(c, to), device_id_type=MESH)
    pl.semaphore_wait(barrier, len(columns) + len(partners))


def send(src, dst, send_sem, recv_sem, device):
    return pltpu.make_async_remote_copy(
        src_ref=src,
        dst_ref=dst,
        send_sem=send_sem,
        recv_sem=recv_sem,
        device_id=device,
        device_id_type=MESH,
    )


def gather_kernel(
    n_p, n_r, pk_ref, pv_ref, sizes_ref, slot_ref, out_ref, g1, s2, r2, s_1, r_1, s_2, r_2
):
    c, r, columns, partners = places(n_p, n_r)
    g1[c, 0] = pk_ref[0]
    g1[c, 1] = pv_ref[0]
    greet(c, r, columns, partners)

    def first(to, slot):
        return send(g1.at[slot], g1.at[slot], s_1.at[to], r_1.at[slot], (to, r))

    def second(to, slot):
        return send(s2.at[to], r2.at[slot], s_2.at[to], r_2.at[slot], (c, to))

    for to in columns:
        first(to, c).start()
    for to in columns:
        first(to, to).wait_recv()
    for to in partners:
        s2[to] = g1[prompt_of(sizes_ref, slot_ref, n_p, c * n_r + to)]
        second(to, r).start()
    r2[r] = g1[prompt_of(sizes_ref, slot_ref, n_p, c * n_r + r)]
    for to in partners:
        second(to, to).wait_recv()
    out_ref[...] = r2[...]
    for to in columns:
        first(to, c).wait_send()
    for to in partners:
        second(to, r).wait_send()


def sum_kernel(
    n_p, n_r, sa, sizes_ref, slot_ref, gpk_ref, gpv_ref, ra, sb, rb, s_1, r_1, s_2, r_2
):
    c, r, columns, partners = places(n_p, n_r)
    rows = gpk_ref.shape[1]
    width = gpk_ref.shape[2]
    greet(c, r, columns, partners)

    def first(to, slot):
        return send(sa.at[to], ra.at[slot], s_1.at[to], r_1.at[slot], (c, to))

    def second(to, slot):
        return send(sb.at[to], rb.at[slot], s_2.at[to], r_2.at[slot], (to, r))

    for to in partners:
        first(to, r).start()
    ra[r] = sa[r]
    for to in partners:
        first(to, to).wait_recv()
    owners = [prompt_of(sizes_ref, slot_ref, n_p, c * n_r + src) for src in range(n_r)]
    for low in range(0, width, HD):
        lanes = slice(low, low + HD)
        sums = [jnp.zeros((2, rows, HD), F32) for _ in range(n_p)]
        for src in range(n_r):
            term = ra[src, :, :, lanes].astype(F32)
            for p in range(n_p):
                sums[p] = sums[p] + jnp.where(owners[src] == p, term, 0.0)
        for p in range(n_p):
            sb[p, :, :, lanes] = sums[p]
    for to in columns:
        second(to, c).start()
    out = sb[c]
    for to in columns:
        second(to, to).wait_recv()
        out = out + rb[to]
    gpk_ref[0] = out[0]
    gpv_ref[0] = out[1]
    for to in partners:
        first(to, r).wait_send()
    for to in columns:
        second(to, c).wait_send()


def attend_kernel(
    q_hbm,
    do_hbm,
    rk_ref,
    rv_ref,
    own_ref,
    len_ref,
    gq_out,
    grk_ref,
    grv_ref,
    sums_ref,
    q_v,
    do_v,
    gq_v,
    kall,
    vall,
    ktall,
    gk_acc,
    gv_acc,
    s_0,
    s_1,
    d_0,
    d_1,
    p_0,
    p_1,
    ds_0,
    ds_1,
    m_0,
    m_1,
    in_sem,
    out_sem,
):
    n_r, _, rows, _ = own_ref.shape
    kv_heads = kall.shape[0]
    heads = kv_heads * GRP
    tok = q_v.shape[0]
    plen = rows * n_r
    half = tok // 2
    top = plen + half
    keys = plen + tok
    scaling = 1.0 / math.sqrt(HD)
    to_exp2 = scaling * math.log2(math.e)

    def group_lanes(kv):
        return pl.ds(pl.multiple_of(kv * GRP * HD, HD), GRP * HD)

    def queries_in(kv):
        lanes = group_lanes(kv)
        return pltpu.make_async_copy(q_hbm.at[0, :, lanes], q_v.at[:, lanes], in_sem.at[0, kv])

    def upstream_in(kv):
        lanes = group_lanes(kv)
        return pltpu.make_async_copy(do_hbm.at[0, :, lanes], do_v.at[:, lanes], in_sem.at[1, kv])

    for kv in range(kv_heads):
        queries_in(kv).start()
        upstream_in(kv).start()
    gk_acc[...] = jnp.zeros_like(gk_acc)
    gv_acc[...] = jnp.zeros_like(gv_acc)
    for ref in (p_0, p_1, ds_0, ds_1):
        ref[...] = jnp.zeros_like(ref)
    live_mask = lax.broadcasted_iota(jnp.int32, (tok, HD), 0) < len_ref[0]
    slots = ((s_0, d_0, p_0, ds_0, m_0), (s_1, d_1, p_1, ds_1, m_1))

    def head_lanes(head):
        return pl.ds(pl.multiple_of(head * HD, HD), HD)

    def load_group(kv):
        lanes = head_lanes(kv)
        kall[kv, :plen] = own_ref[:, 0, :, lanes].reshape(plen, HD)
        vall[kv, :plen] = own_ref[:, 1, :, lanes].reshape(plen, HD)
        kall[kv, plen:] = rk_ref[0, :, lanes]
        vall[kv, plen:] = rv_ref[0, :, lanes]
        ktall[kv] = jnp.transpose(kall[kv].astype(F32)).astype(BF16)
        queries_in(kv).wait()
        upstream_in(kv).wait()

        def mask_rows(i, carry):
            cols = head_lanes(kv * GRP + i)
            do_v[:, cols] = jnp.where(live_mask, do_v[:, cols], jnp.zeros((), BF16))
            return carry

        lax.fori_loop(0, GRP, mask_rows, 0)

    def scores(head, slot):
        s_ref, m_ref = slot[0], slot[4]
        s = nt(kall[head // GRP], q_v[:, head_lanes(head)])
        causal = lax.broadcasted_iota(jnp.int32, (half, half), 0) <= lax.broadcasted_iota(
            jnp.int32, (half, half), 1
        )
        s_p = s[:plen]
        s_l = jnp.where(causal, s[plen:top, :half], -jnp.inf)
        s_r = s[plen:top, half:]
        s_b = jnp.where(causal, s[top:, half:], -jnp.inf)
        s_ref[:plen] = s_p
        s_ref[plen:top, :half] = s_l
        s_ref[plen:top, half:] = s_r
        s_ref[top:, half:] = s_b
        m_p = jnp.max(s_p, axis=0, keepdims=True)
        m_l = jnp.max(s_l, axis=0, keepdims=True)
        m_r = jnp.max(jnp.maximum(s_r, s_b), axis=0, keepdims=True)
        m_ref[...] = jnp.maximum(m_p, jnp.concatenate([m_l, m_r], axis=1)) * to_exp2

    def value_products(head, slot):
        slot[1][...] = nt(vall[head // GRP], do_v[:, head_lanes(head)])

    def add_key_grad(head, slot):
        gk_acc[head // GRP] += nn(slot[3][...], q_v[:, head_lanes(head)])

    def add_value_grad(head, slot):
        gv_acc[head // GRP] += nn(slot[2][...], do_v[:, head_lanes(head)])

    def query_grad(head, slot):
        g_t = nn(ktall[head // GRP], slot[3][...]) * scaling
        gq_v[:, head_lanes(head)] = jnp.transpose(g_t).astype(BF16)

    quarter = half // 2

    def blocks(side):
        limit = top if side == 0 else keys
        return [(low, low + quarter) for low in range(0, limit, quarter)]

    def column(side):
        return slice(side * half, (side + 1) * half)

    def fold(x):
        return jnp.sum(x.reshape(-1, 8, half), axis=0)

    def exponentials(slot, side):
        s_ref, d_ref, m_ref = slot[0], slot[1], slot[4]
        cols = column(side)
        m = m_ref[:, cols]
        norm = jnp.zeros((8, half), F32)
        dots = jnp.zeros((8, half), F32)
        for low, high in blocks(side):
            e = jnp.exp2(s_ref[low:high, cols] * to_exp2 - m)
            s_ref[low:high, cols] = e
            norm = norm + fold(e)
            dots = dots + fold(e * d_ref[low:high, cols])
        inv = 1.0 / jnp.sum(norm, axis=0, keepdims=True)
        return inv, jnp.sum(dots, axis=0, keepdims=True) * inv

    def differences(slot, side, inv, dot_row):
        s_ref, d_ref, p_ref, ds_ref = slot[:4]
        cols = column(side)
        for low, high in blocks(side):
            p = s_ref[low:high, cols] * inv
            p_ref[low:high, cols] = p.astype(BF16)
            ds_ref[low:high, cols] = (p * (d_ref[low:high, cols] - dot_row)).astype(BF16)

    def step(head, cur, other):
        ahead = jnp.minimum(head + 1, heads - 1)
        behind = jnp.maximum(head - 1, 0)
        scores(ahead, other)
        stats_0 = exponentials(cur, 0)
        add_key_grad(behind, other)
        stats_1 = exponentials(cur, 1)
        add_value_grad(behind, other)
        differences(cur, 0, *stats_0)
        query_grad(behind, other)
        differences(cur, 1, *stats_1)
        value_products(ahead, other)

    def store_queries(kv):
        lanes = group_lanes(kv)
        return pltpu.make_async_copy(gq_v.at[:, lanes], gq_out.at[0, :, lanes], out_sem.at[kv])

    def store_group(kv):
        lanes = head_lanes(kv)
        grad_k = gk_acc[kv] * scaling
        grad_v = gv_acc[kv]
        sums_ref[:, 0, :, lanes] = grad_k[:plen].astype(BF16).reshape(n_r, rows, HD)
        sums_ref[:, 1, :, lanes] = grad_v[:plen].astype(BF16).reshape(n_r, rows, HD)
        grk_ref[0, :, lanes] = grad_k[plen:].astype(BF16)
        grv_ref[0, :, lanes] = grad_v[plen:].astype(BF16)
        store_queries(kv).start()

    load_group(0)
    scores(0, slots[0])
    value_products(0, slots[0])
    pairs = GRP // 2

    def pair(index, carry):
        kv = index // pairs
        place = index % pairs

        @pl.when((place == pairs - 1) & (kv < kv_heads - 1))
        def _():
            load_group(kv + 1)

        @pl.when((place == 1) & (kv > 0))
        def _():
            store_group(kv - 1)

        step(2 * index, slots[0], slots[1])
        step(2 * index + 1, slots[1], slots[0])
        return carry

    lax.fori_loop(0, heads // 2, pair, 0)
    add_key_grad(heads - 1, slots[1])
    add_value_grad(heads - 1, slots[1])
    query_grad(heads - 1, slots[1])
    store_group(kv_heads - 1)
    for kv in range(kv_heads):
        store_queries(kv).wait()


def per_device(
    queries,
    resp_keys,
    resp_values,
    grad_out,
    prompt_keys,
    prompt_values,
    group_sizes,
    slot_response,
    lengths,
):
    n_p = lax.axis_size("prompt")
    n_r = lax.axis_size("resp")
    tok = queries.shape[1]
    width = queries.shape[2]
    rows = prompt_keys.shape[1]
    kv_width = prompt_keys.shape[2]
    kv_heads = kv_width // HD
    keys = rows * n_r + tok
    vmem = pl.BlockSpec(memory_space=pltpu.VMEM)
    smem = pl.BlockSpec(memory_space=pltpu.SMEM)
    hbm = pl.BlockSpec(memory_space=pltpu.HBM)
    dma = pltpu.SemaphoreType.DMA
    own = pl.pallas_call(
        functools.partial(gather_kernel, n_p, n_r),
        out_shape=jax.ShapeDtypeStruct((n_r, 2, rows, kv_width), BF16),
        in_specs=[vmem, vmem, smem, smem],
        out_specs=vmem,
        scratch_shapes=[
            pltpu.VMEM((n_p, 2, rows, kv_width), BF16),
            pltpu.VMEM((n_r, 2, rows, kv_width), BF16),
            pltpu.VMEM((n_r, 2, rows, kv_width), BF16),
            dma((n_p,)),
            dma((n_p,)),
            dma((n_r,)),
            dma((n_r,)),
        ],
        compiler_params=pltpu.CompilerParams(
            collective_id=0, has_side_effects=True, vmem_limit_bytes=VMEM_LIMIT
        ),
    )(prompt_keys, prompt_values, group_sizes, slot_response)
    grad_q, grad_rk, grad_rv, sums = pl.pallas_call(
        attend_kernel,
        out_shape=(
            jax.ShapeDtypeStruct(queries.shape, BF16),
            jax.ShapeDtypeStruct(resp_keys.shape, BF16),
            jax.ShapeDtypeStruct(resp_values.shape, BF16),
            jax.ShapeDtypeStruct((n_r, 2, rows, kv_width), BF16),
        ),
        in_specs=[hbm, hbm, vmem, vmem, vmem, smem],
        out_specs=(hbm, vmem, vmem, vmem),
        scratch_shapes=[
            pltpu.VMEM((tok, width), BF16),
            pltpu.VMEM((tok, width), BF16),
            pltpu.VMEM((tok, width), BF16),
            pltpu.VMEM((kv_heads, keys, HD), BF16),
            pltpu.VMEM((kv_heads, keys, HD), BF16),
            pltpu.VMEM((kv_heads, HD, keys), BF16),
            pltpu.VMEM((kv_heads, keys, HD), F32),
            pltpu.VMEM((kv_heads, keys, HD), F32),
            pltpu.VMEM((keys, tok), F32),
            pltpu.VMEM((keys, tok), F32),
            pltpu.VMEM((keys, tok), F32),
            pltpu.VMEM((keys, tok), F32),
            pltpu.VMEM((keys, tok), BF16),
            pltpu.VMEM((keys, tok), BF16),
            pltpu.VMEM((keys, tok), BF16),
            pltpu.VMEM((keys, tok), BF16),
            pltpu.VMEM((1, tok), F32),
            pltpu.VMEM((1, tok), F32),
            dma((2, kv_heads)),
            dma((kv_heads,)),
        ],
        compiler_params=pltpu.CompilerParams(vmem_limit_bytes=VMEM_LIMIT),
    )(queries, grad_out, resp_keys, resp_values, own, lengths)
    grad_pk, grad_pv = pl.pallas_call(
        functools.partial(sum_kernel, n_p, n_r),
        out_shape=(
            jax.ShapeDtypeStruct(prompt_keys.shape, F32),
            jax.ShapeDtypeStruct(prompt_values.shape, F32),
        ),
        in_specs=[vmem, smem, smem],
        out_specs=(vmem, vmem),
        scratch_shapes=[
            pltpu.VMEM((n_r, 2, rows, kv_width), BF16),
            pltpu.VMEM((n_p, 2, rows, kv_width), F32),
            pltpu.VMEM((n_p, 2, rows, kv_width), F32),
            dma((n_r,)),
            dma((n_r,)),
            dma((n_p,)),
            dma((n_p,)),
        ],
        compiler_params=pltpu.CompilerParams(
            collective_id=1, has_side_effects=True, vmem_limit_bytes=VMEM_LIMIT
        ),
    )(sums, group_sizes, slot_response)
    return grad_q, grad_rk, grad_rv, grad_pk, grad_pv


def solution(mesh):
    in_specs = (
        P(("prompt", "resp"), None, None),
        P(("prompt", "resp"), None, None),
        P(("prompt", "resp"), None, None),
        P(("prompt", "resp"), None, None),
        P("prompt", "resp", None),
        P("prompt", "resp", None),
        P(),
        P(),
        P(("prompt", "resp")),
    )
    out_specs = (
        P(("prompt", "resp"), None, None),
        P(("prompt", "resp"), None, None),
        P(("prompt", "resp"), None, None),
        P("prompt", "resp", None),
        P("prompt", "resp", None),
    )
    return jax.shard_map(
        per_device, mesh=mesh, in_specs=in_specs, out_specs=out_specs, check_vma=False
    )
```

time: 137 us -> 75.7 us (0.55)
  the two profiles are of different devices: /device:TPU:0 before, /device:TPU:13 now
where the time goes in v3:
time: 75.7 us; the launch traced here: 75.4 us
  Pallas kernels  71.1 us (94%)
  local copies, waits for them, and re-layouts  2.95 us (4%)
  between operations  1.3 us (2%)
    pallas_call x1, Pallas kernels, per_device(): pl.pallas_call(functools.partial(sum_kernel, n_p, n_r), out_shape=(jax.Sh...  24.6 us
    pallas_call x1, Pallas kernels, per_device(): pl.pallas_call(attend_kernel, out_shape=(jax.ShapeDtypeStruct(queries.sha...  23.5 us
    pallas_call x1, Pallas kernels, per_device(): pl.pallas_call(functools.partial(gather_kernel, n_p, n_r), out_shape=jax....  23 us
    unnamed x2, local copies, waits for them, and re-layouts  2.95 us

profile of v3, /device:TPU:13, one launch (start us, length us, event | category | flops | bytes accessed | tf_op | source)
XLA Modules:
  0.0 75.4 jit_solution(16812086514481252701)
XLA Ops:
  1.3 23.0 %shard_map.128.own_ref = bf16[8,2,32,512]{3,2,1,0:T(8,128)(2,1)} custom-call(bf16[1,32,512]{2,1,0:T(8,128)(2,1)} %pk_ref.1, bf16[1,32,512]{2,1,0:T(8,128)(2,1)} %pv_ref.1, s32[4]{0:T(128)} %sizes_ref.3, s32[32]{0:T(128)} %slot_ref.3), custom_call_target="tpu_custom_call" | custom-call | tf_op jit(solution)/shard_map/pallas_call | solution.py:369
  24.3 23.5 %shard_map.129 = (bf16[1,256,4096]{2,1,0:T(8,128)(2,1)}, bf16[1,256,512]{2,1,0:T(8,128)(2,1)}, bf16[1,256,512]{2,1,0:T(8,128)(2,1)}, bf16[8,2,32,512]{3,2,1,0:T(8,128)(2,1)}) custom-call(bf16[1,256,4096]{2,1,0:T(8,128)(2,1)} %q_hbm.1, bf16[1,256,4096]{2,1,0:T(8,128)(2,1)} %do_hbm.1, bf16[1,256,512]{2,1,0:T(8,128)(2,1)} %rk_ref.1, ...), custom_call_target="tpu_custom_call" | custom-call | tf_op jit(solution)/shard_map/pallas_call | solution.py:387
  47.8 24.6 %shard_map.130 = (f32[1,32,512]{2,1,0:T(8,128)}, f32[1,32,512]{2,1,0:T(8,128)}) custom-call(bf16[8,2,32,512]{3,2,1,0:T(8,128)(2,1)} %get-tuple-element.14.sa, s32[4]{0:T(128)} %sizes_ref.3, s32[32]{0:T(128)} %slot_ref.3), custom_call_target="tpu_custom_call" | custom-call | tf_op jit(solution)/shard_map/pallas_call | solution.py:421
  72.4 1.5 %copy.17 = f32[1,32,512]{2,1,0:T(8,128)} copy(f32[1,32,512]{2,1,0:T(8,128)} %get-tuple-element.25) | data formatting | bytes 131072
  73.9 1.5 %copy.18 = f32[1,32,512]{2,1,0:T(8,128)} copy(f32[1,32,512]{2,1,0:T(8,128)} %get-tuple-element.26) | data formatting | bytes 131072

commit v4 on v2

--- a/solution.py
+++ b/solution.py
@@ -47,6 +47,7 @@
     sizes_ref,
     slot_ref,
     len_ref,
+    own,
     g1,
     s2,
     r2,
@@ -83,7 +84,7 @@
 ):
     c = lax.axis_index("prompt")
     r = lax.axis_index("resp")
-    rows = g1.shape[2]
+    rows = g1.shape[3]
     kv_heads = kall.shape[0]
     heads = kv_heads * GRP
     tok = q_v.shape[0]
@@ -110,8 +111,8 @@
         return found
 
     first = [
-        pltpu.make_async_copy(pk_hbm.at[0], g1.at[c, 0], in_sem.at[0]),
-        pltpu.make_async_copy(pv_hbm.at[0], g1.at[c, 1], in_sem.at[1]),
+        pltpu.make_async_copy(pk_hbm.at[0], own.at[0], in_sem.at[0]),
+        pltpu.make_async_copy(pv_hbm.at[0], own.at[1], in_sem.at[1]),
         pltpu.make_async_copy(sizes_hbm, sizes_ref, in_sem.at[2]),
         pltpu.make_async_copy(slot_hbm, slot_ref, in_sem.at[3]),
         pltpu.make_async_copy(len_hbm, len_ref, in_sem.at[4]),
@@ -141,14 +142,16 @@
         pl.semaphore_signal(barrier, inc=1, device_id=(c, row_peer(i)), device_id_type=MESH)
     for copy in first:
         copy.wait()
+    for kv in range(kv_heads):
+        g1[kv, c] = own[:, :, kv * HD : (kv + 1) * HD]
     pl.semaphore_wait(barrier, n_p + n_r - 2)
 
-    def gather_first(to, slot):
+    def gather_first(kv, to, slot):
         return pltpu.make_async_remote_copy(
-            src_ref=g1.at[slot],
-            dst_ref=g1.at[slot],
-            send_sem=g1_send.at[to],
-            recv_sem=g1_recv.at[slot],
+            src_ref=g1.at[kv, slot],
+            dst_ref=g1.at[kv, slot],
+            send_sem=g1_send.at[kv, to],
+            recv_sem=g1_recv.at[kv, slot],
             device_id=(to, r),
             device_id_type=MESH,
         )
@@ -183,22 +186,34 @@
             device_id_type=MESH,
         )
 
-    for i in range(1, n_p):
-        gather_first(column_peer(i), c).start()
+    def send_first(kv):
+        for i in range(1, n_p):
+            gather_first(kv, column_peer(i), c).start()
+
+    def picked(kv, to):
+        owner = prompt_of(to)
+        block = g1[kv, 0]
+        for p in range(1, n_p):
+            block = jnp.where(owner == p, g1[kv, p], block)
+        return block
+
+    def send_second(kv):
+        for i in range(1, n_p):
+            gather_first(kv, column_peer(i), column_peer(i)).wait_recv()
+        for i in range(1, n_r):
+            to = row_peer(i)
+            s2[kv, to] = picked(kv, to)
+            gather_second(kv, to, r).start()
+        r2[kv, r] = picked(kv, r)
+
+    send_first(0)
+    send_second(0)
+    for kv in range(1, kv_heads):
+        send_first(kv)
     gk_acc[...] = jnp.zeros_like(gk_acc)
     gv_acc[...] = jnp.zeros_like(gv_acc)
     for ref in (p_0, p_1, ds_0, ds_1):
         ref[...] = jnp.zeros_like(ref)
-    for i in range(1, n_p):
-        gather_first(column_peer(i), column_peer(i)).wait_recv()
-    for kv in range(kv_heads):
-        lanes = slice(kv * HD, (kv + 1) * HD)
-        for i in range(1, n_r):
-            to = row_peer(i)
-            s2[kv, to] = g1[prompt_of(to), :, :, lanes]
-            gather_second(kv, to, r).start()
-        r2[kv, r] = g1[prompt_of(r), :, :, lanes]
-
     do_in.wait()
     live_mask = lax.broadcasted_iota(jnp.int32, (tok, HD), 0) < len_ref[0]
 
@@ -220,6 +235,11 @@
     def load_keys(kv):
         for i in range(1, n_r):
             gather_second(kv, row_peer(i), row_peer(i)).wait_recv()
+
+        @pl.when(kv < kv_heads - 1)
+        def _():
+            send_second(kv + 1)
+
         kall[kv, :plen] = r2[kv, :, 0].reshape(plen, HD)
         vall[kv, :plen] = r2[kv, :, 1].reshape(plen, HD)
         ktall[kv] = jnp.transpose(kall[kv].astype(F32)).astype(BF16)
@@ -343,7 +363,7 @@
         gpk_ref[0, :, lanes] = out[0]
         gpv_ref[0, :, lanes] = out[1]
 
-    load_keys(0)
+    load_keys(jnp.int32(0))
     scores(0, slots[0])
     value_products(0, slots[0])
     pairs = GRP // 2
@@ -378,10 +398,10 @@
     combine(kv_heads - 1)
     finish(kv_heads - 1)
 
-    for i in range(1, n_p):
-        gather_first(column_peer(i), c).wait_send()
     for kv in range(kv_heads):
         store_queries(kv).wait()
+        for i in range(1, n_p):
+            gather_first(kv, column_peer(i), c).wait_send()
         for i in range(1, n_r):
             gather_second(kv, row_peer(i), r).wait_send()
             sum_first(kv, row_peer(i), r).wait_send()
@@ -389,16 +409,33 @@
             sum_second(kv, column_peer(i), c).wait_send()
 
 
-def store_kernel(*refs):
-    count = (len(refs) - 1) // 2
-    sem = refs[-1]
-    copies = [
-        pltpu.make_async_copy(refs[k], refs[count + k], sem.at[k]) for k in range(count)
-    ]
-    for copy in copies:
-        copy.start()
-    for copy in copies:
-        copy.wait()
+def store_kernel(pieces, *refs):
+    count = len(pieces)
+    sources, targets, staged = refs[:count], refs[count : 2 * count], refs[2 * count : 3 * count]
+    in_sem, out_sem = refs[3 * count :]
+    loads, stores = [], []
+    for k, parts in enumerate(pieces):
+        size = sources[k].shape[1] // parts
+        for part in range(parts):
+            rows = pl.ds(part * size, size)
+            place = len(loads)
+            loads.append(
+                pltpu.make_async_copy(
+                    sources[k].at[:, rows], staged[k].at[:, rows], in_sem.at[place]
+                )
+            )
+            stores.append(
+                pltpu.make_async_copy(
+                    staged[k].at[:, rows], targets[k].at[:, rows], out_sem.at[place]
+                )
+            )
+    for load in loads:
+        load.start()
+    for load, store in zip(loads, stores):
+        load.wait()
+        store.start()
+    for store in stores:
+        store.wait()
 
 
 def per_device(
@@ -443,7 +480,8 @@
             pltpu.SMEM(group_sizes.shape, jnp.int32),
             pltpu.SMEM(slot_response.shape, jnp.int32),
             pltpu.SMEM(lengths.shape, jnp.int32),
-            pltpu.VMEM((n_p, 2, rows, kv_width), BF16),
+            pltpu.VMEM((2, rows, kv_width), BF16),
+            pltpu.VMEM((kv_heads, n_p, 2, rows, HD), BF16),
             pltpu.VMEM((kv_heads, n_r, 2, rows, HD), BF16),
             pltpu.VMEM((kv_heads, n_r, 2, rows, HD), BF16),
             pltpu.VMEM((kv_heads, n_r, 2, rows, HD), BF16),
@@ -468,8 +506,8 @@
             dma((7,)),
             dma((2, kv_heads)),
             dma((kv_heads,)),
-            dma((n_p,)),
-            dma((n_p,)),
+            dma((kv_heads, n_p)),
+            dma((kv_heads, n_p)),
             dma((kv_heads, n_r)),
             dma((kv_heads, n_r)),
             dma((kv_heads, n_r)),
@@ -496,12 +534,14 @@
         slot_response,
         lengths,
     )
+    pieces = (4, 1, 1, 1, 1)
     return pl.pallas_call(
-        store_kernel,
+        functools.partial(store_kernel, pieces),
         out_shape=out_shape,
-        in_specs=[anywhere] * len(out_shape),
+        in_specs=[hbm] * len(out_shape),
         out_specs=(hbm,) * len(out_shape),
-        scratch_shapes=[dma((len(out_shape),))],
+        scratch_shapes=[pltpu.VMEM(out.shape, out.dtype) for out in out_shape]
+        + [dma((sum(pieces),)), dma((sum(pieces),))],
         compiler_params=pltpu.CompilerParams(vmem_limit_bytes=VMEM_LIMIT),
     )(*results)
 

time: 137 us -> 57.5 us (0.42)
  Pallas kernels: 136 us -> 56 us
    pallas_call x1, Pallas kernels: 84.5 us -> 2.7 us  [per_device(): pl.pallas_call(functools.partial(store_kernel, pieces), out_shape=out_sha...]
    pallas_call x1, Pallas kernels: 51.5 us -> 53.3 us  [per_device(): pl.pallas_call(functools.partial(kernel, n_p, n_r), out_shape=out_shape,...]
where the time goes in v4:
time: 57.5 us; the launch traced here: 57.3 us
  Pallas kernels  56 us (97%)
  between operations  1.29 us (2%)
    pallas_call x1, Pallas kernels, per_device(): pl.pallas_call(functools.partial(kernel, n_p, n_r), out_shape=out_shape,...  53.3 us
    pallas_call x1, Pallas kernels, per_device(): pl.pallas_call(functools.partial(store_kernel, pieces), out_shape=out_sha...  2.7 us

profile of v4, /device:TPU:0, one launch (start us, length us, event | category | flops | bytes accessed | tf_op | source)
XLA Modules:
  0.0 57.3 jit_solution(6207778428672912664)
XLA Ops:
  1.3 53.3 %shard_map.128 = (bf16[1,256,4096]{2,1,0:T(8,128)(2,1)}, bf16[1,256,512]{2,1,0:T(8,128)(2,1)}, bf16[1,256,512]{2,1,0:T(8,128)(2,1)}, f32[1,32,512]{2,1,0:T(8,128)}, f32[1,32,512]{2,1,0:T(8,128)}) custom-call(bf16[1,256,4096]{2,1,0:T(8,128)(2,1)} %q_hbm.1, bf16[1,256,4096]{2,1,0:T(8,128)(2,1)} %do_hbm.1, bf16[1,256,512]{2,1,0:T(8,128)(2,1)} %rk_hbm.1, ...), custom_call_target="tpu_custom_call" | custom-call | flops 5368709120 | bytes 8388608 | tf_op jit(solution)/shard_map/pallas_call | solution.py:471
  54.6 2.7 %shard_map.129 = (bf16[1,256,4096]{2,1,0:T(8,128)(2,1)}, bf16[1,256,512]{2,1,0:T(8,128)(2,1)}, bf16[1,256,512]{2,1,0:T(8,128)(2,1)}, f32[1,32,512]{2,1,0:T(8,128)}, f32[1,32,512]{2,1,0:T(8,128)}) custom-call(bf16[1,256,4096]{2,1,0:T(8,128)(2,1)} %get-tuple-element.10.refs_0_, bf16[1,256,512]{2,1,0:T(8,128)(2,1)} %get-tuple-element.11.refs_1_, ...), custom_call_target="tpu_custom_call" | custom-call | tf_op jit(solution)/shard_map/pallas_call | solution.py:538

commit v5 on v4

--- a/solution.py
+++ b/solution.py
@@ -235,11 +235,6 @@
     def load_keys(kv):
         for i in range(1, n_r):
             gather_second(kv, row_peer(i), row_peer(i)).wait_recv()
-
-        @pl.when(kv < kv_heads - 1)
-        def _():
-            send_second(kv + 1)
-
         kall[kv, :plen] = r2[kv, :, 0].reshape(plen, HD)
         vall[kv, :plen] = r2[kv, :, 1].reshape(plen, HD)
         ktall[kv] = jnp.transpose(kall[kv].astype(F32)).astype(BF16)
@@ -363,7 +358,9 @@
         gpk_ref[0, :, lanes] = out[0]
         gpv_ref[0, :, lanes] = out[1]
 
-    load_keys(jnp.int32(0))
+    load_keys(0)
+    if kv_heads > 1:
+        send_second(1)
     scores(0, slots[0])
     value_products(0, slots[0])
     pairs = GRP // 2
@@ -380,9 +377,13 @@
         def _():
             send_sums(kv - 1)
 
-        @pl.when((place == pairs - 1) & (kv > 0))
+        @pl.when((place == 1) & (kv > 1))
         def _():
-            combine(kv - 1)
+            combine(kv - 2)
+
+        @pl.when((place == 2) & (kv < kv_heads - 2))
+        def _():
+            send_second(kv + 2)
 
         step(2 * index, slots[0], slots[1])
         step(2 * index + 1, slots[1], slots[0])
@@ -393,10 +394,13 @@
     add_value_grad(heads - 1, slots[1])
     query_grad(heads - 1, slots[1])
     send_sums(kv_heads - 1)
-    for kv in range(kv_heads - 1):
+    if kv_heads > 1:
+        combine(kv_heads - 2)
+    for kv in range(kv_heads - 2):
         finish(kv)
     combine(kv_heads - 1)
-    finish(kv_heads - 1)
+    for kv in range(max(kv_heads - 2, 0), kv_heads):
+        finish(kv)
 
     for kv in range(kv_heads):
         store_queries(kv).wait()

time: 57.5 us -> 49.7 us (0.86)
  Pallas kernels: 56 us -> 48.2 us
    pallas_call x1, Pallas kernels: 53.3 us -> 45.5 us  [per_device(): pl.pallas_call(functools.partial(kernel, n_p, n_r), out_shape=out_shape,...]
where the time goes in v5:
time: 49.7 us; the launch traced here: 49.5 us
  Pallas kernels  48.2 us (97%)
  between operations  1.29 us (3%)
    pallas_call x1, Pallas kernels, per_device(): pl.pallas_call(functools.partial(kernel, n_p, n_r), out_shape=out_shape,...  45.5 us
    pallas_call x1, Pallas kernels, per_device(): pl.pallas_call(functools.partial(store_kernel, pieces), out_shape=out_sha...  2.7 us

profile of v5, /device:TPU:0, one launch (start us, length us, event | category | flops | bytes accessed | tf_op | source)
XLA Modules:
  0.0 49.5 jit_solution(6618671379000138333)
XLA Ops:
  1.3 45.5 %shard_map.128 = (bf16[1,256,4096]{2,1,0:T(8,128)(2,1)}, bf16[1,256,512]{2,1,0:T(8,128)(2,1)}, bf16[1,256,512]{2,1,0:T(8,128)(2,1)}, f32[1,32,512]{2,1,0:T(8,128)}, f32[1,32,512]{2,1,0:T(8,128)}) custom-call(bf16[1,256,4096]{2,1,0:T(8,128)(2,1)} %q_hbm.1, bf16[1,256,4096]{2,1,0:T(8,128)(2,1)} %do_hbm.1, bf16[1,256,512]{2,1,0:T(8,128)(2,1)} %rk_hbm.1, ...), custom_call_target="tpu_custom_call" | custom-call | flops 5368709120 | bytes 8388608 | tf_op jit(solution)/shard_map/pallas_call | solution.py:475
  46.8 2.7 %shard_map.129 = (bf16[1,256,4096]{2,1,0:T(8,128)(2,1)}, bf16[1,256,512]{2,1,0:T(8,128)(2,1)}, bf16[1,256,512]{2,1,0:T(8,128)(2,1)}, f32[1,32,512]{2,1,0:T(8,128)}, f32[1,32,512]{2,1,0:T(8,128)}) custom-call(bf16[1,256,4096]{2,1,0:T(8,128)(2,1)} %get-tuple-element.10.refs_0_, bf16[1,256,512]{2,1,0:T(8,128)(2,1)} %get-tuple-element.11.refs_1_, ...), custom_call_target="tpu_custom_call" | custom-call | tf_op jit(solution)/shard_map/pallas_call | solution.py:542

commit v6 on v5

--- a/solution.py
+++ b/solution.py
@@ -53,6 +53,7 @@
     r2,
     sa,
     ra,
+    kept,
     sb,
     rb,
     kall,
@@ -329,7 +330,6 @@
         lanes = head_lanes(kv)
         grk_ref[0, :, lanes] = grad_k[plen:].astype(BF16)
         grv_ref[0, :, lanes] = grad_v[plen:].astype(BF16)
-        store_queries(kv).start()
 
     def store_queries(kv):
         cols = pl.ds(pl.multiple_of(kv * GRP * HD, HD), GRP * HD)
@@ -345,16 +345,17 @@
             for p in range(n_p):
                 sums[p] = sums[p] + jnp.where(owner == p, term, 0.0)
         for p in range(n_p):
-            sb[kv, p] = sums[p]
+            kept[kv, p] = sums[p]
+            sb[kv, p] = sums[p].astype(BF16)
         for i in range(1, n_p):
             sum_second(kv, column_peer(i), c).start()
 
     def finish(kv):
         lanes = head_lanes(kv)
-        out = sb[kv, c]
+        out = kept[kv, c]
         for i in range(1, n_p):
             sum_second(kv, column_peer(i), column_peer(i)).wait_recv()
-            out = out + rb[kv, column_peer(i)]
+            out = out + rb[kv, column_peer(i)].astype(F32)
         gpk_ref[0, :, lanes] = out[0]
         gpv_ref[0, :, lanes] = out[1]
 
@@ -376,6 +377,7 @@
         @pl.when((place == 1) & (kv > 0))
         def _():
             send_sums(kv - 1)
+            store_queries(kv - 1).start()
 
         @pl.when((place == 1) & (kv > 1))
         def _():
@@ -392,8 +394,9 @@
     lax.fori_loop(0, heads // 2, pair, 0)
     add_key_grad(heads - 1, slots[1])
     add_value_grad(heads - 1, slots[1])
+    send_sums(kv_heads - 1)
     query_grad(heads - 1, slots[1])
-    send_sums(kv_heads - 1)
+    store_queries(kv_heads - 1).start()
     if kv_heads > 1:
         combine(kv_heads - 2)
     for kv in range(kv_heads - 2):
@@ -491,7 +494,8 @@
             pltpu.VMEM((kv_heads, n_r, 2, rows, HD), BF16),
             pltpu.VMEM((kv_heads, n_r, 2, rows, HD), BF16),
             pltpu.VMEM((kv_heads, n_p, 2, rows, HD), F32),
-            pltpu.VMEM((kv_heads, n_p, 2, rows, HD), F32),
+            pltpu.VMEM((kv_heads, n_p, 2, rows, HD), BF16),
+            pltpu.VMEM((kv_heads, n_p, 2, rows, HD), BF16),
             pltpu.VMEM((kv_heads, keys, HD), BF16),
             pltpu.VMEM((kv_heads, keys, HD), BF16),
             pltpu.VMEM((kv_heads, HD, keys), BF16),
@@ -538,7 +542,7 @@
         slot_response,
         lengths,
     )
-    pieces = (4, 1, 1, 1, 1)
+    pieces = (8, 2, 2, 1, 1)
     return pl.pallas_call(
         functools.partial(store_kernel, pieces),
         out_shape=out_shape,

time: 49.7 us -> 49.4 us (level)
  no operation moved by 1% of the time
where the time goes in v6:
time: 49.4 us; the launch traced here: 49.2 us
  Pallas kernels  47.9 us (97%)
  between operations  1.29 us (3%)
    pallas_call x1, Pallas kernels, per_device(): pl.pallas_call(functools.partial(kernel, n_p, n_r), out_shape=out_shape,...  45.2 us
    pallas_call x1, Pallas kernels, per_device(): pl.pallas_call(functools.partial(store_kernel, pieces), out_shape=out_sha...  2.71 us

profile of v6, /device:TPU:0, one launch (start us, length us, event | category | flops | bytes accessed | tf_op | source)
XLA Modules:
  0.0 49.2 jit_solution(329615296955279051)
XLA Ops:
  1.3 45.2 %shard_map.128 = (bf16[1,256,4096]{2,1,0:T(8,128)(2,1)}, bf16[1,256,512]{2,1,0:T(8,128)(2,1)}, bf16[1,256,512]{2,1,0:T(8,128)(2,1)}, f32[1,32,512]{2,1,0:T(8,128)}, f32[1,32,512]{2,1,0:T(8,128)}) custom-call(bf16[1,256,4096]{2,1,0:T(8,128)(2,1)} %q_hbm.1, bf16[1,256,4096]{2,1,0:T(8,128)(2,1)} %do_hbm.1, bf16[1,256,512]{2,1,0:T(8,128)(2,1)} %rk_hbm.1, ...), custom_call_target="tpu_custom_call" | custom-call | flops 5368709120 | bytes 8388608 | tf_op jit(solution)/shard_map/pallas_call | solution.py:478
  46.5 2.7 %shard_map.129 = (bf16[1,256,4096]{2,1,0:T(8,128)(2,1)}, bf16[1,256,512]{2,1,0:T(8,128)(2,1)}, bf16[1,256,512]{2,1,0:T(8,128)(2,1)}, f32[1,32,512]{2,1,0:T(8,128)}, f32[1,32,512]{2,1,0:T(8,128)}) custom-call(bf16[1,256,4096]{2,1,0:T(8,128)(2,1)} %get-tuple-element.10.refs_0_, bf16[1,256,512]{2,1,0:T(8,128)(2,1)} %get-tuple-element.11.refs_1_, ...), custom_call_target="tpu_custom_call" | custom-call | tf_op jit(solution)/shard_map/pallas_call | solution.py:546

commit v7 on v5

--- a/solution.py
+++ b/solution.py
@@ -358,9 +358,9 @@
         gpk_ref[0, :, lanes] = out[0]
         gpv_ref[0, :, lanes] = out[1]
 
-    load_keys(0)
     if kv_heads > 1:
         send_second(1)
+    load_keys(0)
     scores(0, slots[0])
     value_products(0, slots[0])
     pairs = GRP // 2

time: 49.7 us -> 49.6 us (level)
  no operation moved by 1% of the time
where the time goes in v7:
time: 49.6 us; the launch traced here: 49.5 us
  Pallas kernels  48.2 us (97%)
  between operations  1.29 us (3%)
    pallas_call x1, Pallas kernels, per_device(): pl.pallas_call(functools.partial(kernel, n_p, n_r), out_shape=out_shape,...  45.5 us
    pallas_call x1, Pallas kernels, per_device(): pl.pallas_call(functools.partial(store_kernel, pieces), out_shape=out_sha...  2.7 us

profile of v7, /device:TPU:0, one launch (start us, length us, event | category | flops | bytes accessed | tf_op | source)
XLA Modules:
  0.0 49.5 jit_solution(17501741619303322325)
XLA Ops:
  1.3 45.5 %shard_map.128 = (bf16[1,256,4096]{2,1,0:T(8,128)(2,1)}, bf16[1,256,512]{2,1,0:T(8,128)(2,1)}, bf16[1,256,512]{2,1,0:T(8,128)(2,1)}, f32[1,32,512]{2,1,0:T(8,128)}, f32[1,32,512]{2,1,0:T(8,128)}) custom-call(bf16[1,256,4096]{2,1,0:T(8,128)(2,1)} %q_hbm.1, bf16[1,256,4096]{2,1,0:T(8,128)(2,1)} %do_hbm.1, bf16[1,256,512]{2,1,0:T(8,128)(2,1)} %rk_hbm.1, ...), custom_call_target="tpu_custom_call" | custom-call | flops 5368709120 | bytes 8388608 | tf_op jit(solution)/shard_map/pallas_call | solution.py:475
  46.8 2.7 %shard_map.129 = (bf16[1,256,4096]{2,1,0:T(8,128)(2,1)}, bf16[1,256,512]{2,1,0:T(8,128)(2,1)}, bf16[1,256,512]{2,1,0:T(8,128)(2,1)}, f32[1,32,512]{2,1,0:T(8,128)}, f32[1,32,512]{2,1,0:T(8,128)}) custom-call(bf16[1,256,4096]{2,1,0:T(8,128)(2,1)} %get-tuple-element.10.refs_0_, bf16[1,256,512]{2,1,0:T(8,128)(2,1)} %get-tuple-element.11.refs_1_, ...), custom_call_target="tpu_custom_call" | custom-call | tf_op jit(solution)/shard_map/pallas_call | solution.py:542
